TPU v7x, 512 devices: a whole 4x4x16 slice. The times are simulated.
512 devices in a mesh: kv: 8 (over y, core), ctx: 64 (over x, z).
Axes of the slice: x: 4, y: 4, z: 16, core: 2. Of those that a mesh axis runs over, the one named last changes fastest.
Arguments:
- queries: bfloat16 [128, 16384], P('ctx', 'kv'), may hold values from -30 to 30
- cache_keys: bfloat16 [131072, 1024], P('ctx', 'kv'), may hold values from -12 to 12
- cache_values: bfloat16 [131072, 1024], P('ctx', 'kv'), may hold values from -6 to 6
- out_weight: bfloat16 [16384, 16384], P('kv', 'ctx'), may hold values from -0.046875 to 0.046875
- cached_length: int32 [1], replicated, may hold values from 124928 to 126975
- start: int32 [1], replicated, may hold values from 129024 to 130944
Outputs:
- projected: bfloat16 [128, 16384], P('kv', 'ctx')
All inputs are finite; a program needn't handle non-finite values.
Results may differ from a plain program's by a relative error of at most 0.0049.
Values may be sent and summed in bfloat16 or wider, within the bound.
No kernel may reach another device: no remote copies, remote signals or barrier semaphores. Data moves between devices by JAX's collectives and lax.ppermute only.
A program may use at most 64 MiB of HBM per device.

v0:
```python
import math

import jax
import jax.numpy as jnp
from jax import lax
from jax.sharding import PartitionSpec as P

HD = 128
GROUP = 16


floor_score = -1e30


def shard_partial(query_rows, keys, values, key_base, cached_end, span_start):
    row_count = query_rows.shape[0]
    key_count = keys.shape[0]
    local_groups = keys.shape[1] // HD
    query_heads = query_rows.reshape(row_count, local_groups, GROUP, HD)
    block_len = min(512, key_count)
    block_count = key_count // block_len
    key_blocks = keys.reshape(block_count, block_len, local_groups, HD)
    value_blocks = values.reshape(block_count, block_len, local_groups, HD)
    score_scale = 1.0 / math.sqrt(HD)
    token_ids = jnp.arange(row_count, dtype=jnp.int32)[:, None]

    def advance(state, block_item):
        run_max, run_sum, run_out = state
        key_block, value_block, block_id = block_item
        scores = (
            jnp.einsum("tkgd,skd->tkgs", query_heads, key_block, preferred_element_type=jnp.float32)
            * score_scale
        )
        key_pos = key_base + block_id * block_len + jnp.arange(block_len, dtype=jnp.int32)[None, :]
        visible = (key_pos < cached_end) | (key_pos >= span_start) & (
            key_pos <= span_start + token_ids
        )
        visible = visible[:, None, None, :]
        block_max = jnp.max(jnp.where(visible, scores, floor_score), axis=-1)
        weights = jnp.where(visible, jnp.exp(scores - block_max[..., None]), 0.0)
        block_sum = jnp.sum(weights, axis=-1)
        block_out = jnp.einsum(
            "tkgs,skd->tkgd",
            weights.astype(jnp.bfloat16),
            value_block,
            preferred_element_type=jnp.float32,
        )
        new_max = jnp.maximum(run_max, block_max)
        keep_old = jnp.exp(run_max - new_max)
        keep_new = jnp.exp(block_max - new_max)
        run_sum = run_sum * keep_old + block_sum * keep_new
        run_out = run_out * keep_old[..., None] + block_out * keep_new[..., None]
        return ((new_max, run_sum, run_out), None)

    init_state = (
        jnp.full((row_count, local_groups, GROUP), floor_score, jnp.float32),
        jnp.zeros((row_count, local_groups, GROUP), jnp.float32),
        jnp.zeros((row_count, local_groups, GROUP, HD), jnp.float32),
    )
    block_ids = jnp.arange(block_count, dtype=jnp.int32)
    final_state, unused = lax.scan(advance, init_state, (key_blocks, value_blocks, block_ids))
    return final_state


def finish_rows(attention_part, out_weight):
    return jnp.dot(
        lax.all_gather(attention_part, "ctx", axis=0, tiled=True),
        out_weight,
        preferred_element_type=jnp.float32,
    )


def per_device(queries, cache_keys, cache_values, out_weight, cached_length, start):
    ctx_index = lax.axis_index("ctx")
    key_count = cache_keys.shape[0]
    own_tokens = queries.shape[0]
    key_base = ctx_index * key_count
    all_queries = lax.all_gather(queries, "ctx", axis=0, tiled=True)
    total_tokens = all_queries.shape[0]
    part_max, part_sum, part_out = shard_partial(
        all_queries, cache_keys, cache_values, key_base, cached_length[0], start[0]
    )
    head_count = part_max.shape[1] * part_max.shape[2]
    sent_out = part_out.reshape(total_tokens, 1, head_count * HD)
    came_out, came_max, came_sum = (
        lax.all_to_all(sent_out, "ctx", split_axis=0, concat_axis=1, tiled=True),
        lax.all_to_all(part_max, "ctx", split_axis=0, concat_axis=1, tiled=True),
        lax.all_to_all(part_sum, "ctx", split_axis=0, concat_axis=1, tiled=True),
    )
    shard_count = came_max.shape[1]
    peak_rows = jnp.max(came_max, axis=1, keepdims=True)
    rescale = jnp.exp(came_max - peak_rows)
    numerator = jnp.sum(
        came_out.reshape(own_tokens, shard_count, head_count, HD) * rescale[..., None], axis=1
    )
    denominator = jnp.sum(came_sum * rescale, axis=1)
    attention_part = (
        (numerator / denominator[..., None])
        .reshape(own_tokens, head_count * HD)
        .astype(jnp.bfloat16)
    )
    partial_out = finish_rows(attention_part, out_weight)
    return lax.psum_scatter(partial_out, "kv", scatter_dimension=0, tiled=True).astype(jnp.bfloat16)


def solution(mesh):
    return jax.shard_map(
        per_device,
        mesh=mesh,
        in_specs=(P("ctx", "kv"), P("ctx", "kv"), P("ctx", "kv"), P("kv", "ctx"), P(), P()),
        out_specs=P("kv", "ctx"),
        check_vma=False,
    )
```

profile of v0, /device:TPU:1, one launch (start us, length us, event | category | flops | bytes accessed | tf_op | source)
XLA Modules:
  0.0 384.6 jit_solution(6050901206183625623)
XLA Ops:
  6.5 81.4 %all-gather = bf16[64,2,2048]{2,1,0:T(2,128)(2,1)S(1)} all-gather(bf16[1,2,2048]{2,1,0:T(2,128)(2,1)} %bitcast.155), channel_id=1, replica_groups=mesh['kv'=8,'ctx'=64] {'ctx'}, dimensions={0}, use_global_device_ids=true | all-gather | bytes 532480 | tf_op jit(solution)/shard_map/all_gather | solution.py:78
  88.5 46.3 %while.15 = (s32[]{:T(128)}, f32[128,1,16]{0,2,1:T(8,128)S(1)}, f32[128,1,16]{0,2,1:T(8,128)S(1)}, f32[128,1,16,128]{0,3,2,1:T(8,128)S(1)}, s32[4]{0:T(128)S(1)}...) while((s32[]{:T(128)}, f32[128,1,16]{0,2,1:T(8,128)S(1)}, ...), condition=%wide.region_3.4_spmd.clone, body=%wide.region_0.3_spmd.clone.sunk | while | flops 549668992 | bytes 32669924 | solution.py:61
  89.8 1.3 fusion.57
  92.1 1.6 fusion.58
  93.7 1.9 copy-done.1
  95.7 0.9 fusion.60
  96.6 3.4 fusion.62
  101.4 1.3 fusion.57
  103.7 1.6 fusion.58
  105.3 1.9 copy-done.1
  107.2 0.9 fusion.60
  108.2 3.4 fusion.62
  113.0 1.3 fusion.57
  115.2 1.6 fusion.58
  116.9 1.9 copy-done.1
  119.7 3.4 fusion.62
  124.6 1.3 fusion.57
  126.8 1.6 fusion.58
  128.5 1.9 copy-done.1
  131.3 3.4 fusion.62
  135.5 9.3 %all-to-all-start.1 = ((f32[128,1,16]{2,1,0:T(1,128)}), f32[128,1,16]{2,1,0:T(1,128)S(1)}, u32[]{:S(2)}, u32[]{:S(2)}) async-start(f32[128,1,16]{2,1,0:T(1,128)} %copy.18), calls=%async_computation.1 | async-start | bytes 131072 | tf_op jit(solution)/shard_map/all_to_all | solution.py:87
  145.5 12.8 %all-to-all-done.1 = f32[128,1,16]{2,1,0:T(1,128)S(1)} async-done(((f32[128,1,16]{2,1,0:T(1,128)}), f32[128,1,16]{2,1,0:T(1,128)S(1)}, u32[]{:S(2)}, u32[]{:S(2)}) %all-to-all-start.1) | async-done | bytes 8224 | tf_op jit(solution)/shard_map/all_to_all | solution.py:87
  158.3 4.6 %all-to-all-start.2 = ((f32[128,1,16]{2,1,0:T(1,128)}), f32[128,1,16]{2,1,0:T(1,128)S(1)}, u32[]{:S(2)}, u32[]{:S(2)}) async-start(f32[128,1,16]{2,1,0:T(1,128)} %copy.19), calls=%async_computation.2 | async-start | bytes 131072 | tf_op jit(solution)/shard_map/all_to_all | solution.py:88
  162.9 1.9 copy.17
  164.8 11.6 %all-to-all-done.2 = f32[128,1,16]{2,1,0:T(1,128)S(1)} async-done(((f32[128,1,16]{2,1,0:T(1,128)}), f32[128,1,16]{2,1,0:T(1,128)S(1)}, u32[]{:S(2)}, u32[]{:S(2)}) %all-to-all-start.2) | async-done | bytes 8224 | tf_op jit(solution)/shard_map/all_to_all | solution.py:88
  176.4 4.7 %all-to-all-start = ((f32[128,1,2048]{2,1,0:T(1,128)}), f32[128,1,2048]{2,1,0:T(1,128)S(1)}, u32[]{:S(2)}, u32[]{:S(2)}) async-start(f32[128,1,2048]{2,1,0:T(1,128)} %copy.17), calls=%async_computation | async-start | bytes 2097152 | tf_op jit(solution)/shard_map/all_to_all | solution.py:86
  181.4 32.9 %all-to-all-done = f32[128,1,2048]{2,1,0:T(1,128)S(1)} async-done(((f32[128,1,2048]{2,1,0:T(1,128)}), f32[128,1,2048]{2,1,0:T(1,128)S(1)}, u32[]{:S(2)}, u32[]{:S(2)}) %all-to-all-start) | async-done | bytes 1048608 | tf_op jit(solution)/shard_map/all_to_all | solution.py:86
  214.6 2.0 multiply_reduce_fusion
  216.7 77.2 %all-gather.1 = bf16[64,2,2048]{2,1,0:T(2,128)(2,1)S(1)} all-gather(bf16[1,2,2048]{2,1,0:T(2,128)(2,1)S(1)} %fusion.41), channel_id=1, replica_groups=mesh['kv'=8,'ctx'=64] {'ctx'}, dimensions={0}, use_global_device_ids=true | all-gather | bytes 532480 | tf_op jit(solution)/shard_map/all_gather | solution.py:67
  294.0 0.9 fusion.42
  295.0 81.4 %reduce-scatter.2.cloned.1.call-done = f32[16,256]{1,0:T(8,128)} async-done(((f32[128,256]{1,0:T(8,128)}), f32[16,256]{1,0:T(8,128)}) %reduce-scatter.2.cloned.1.call-update) | async-done | bytes 16400 | tf_op jit(solution)/shard_map/reduce_scatter | solution.py:103
  376.4 1.3 convert_element_type.10
  (52 shorter events, 11.0 us)
Async XLA Ops:
  6.5 287.5 %copy-start = (bf16[2048,256]{1,0:T(8,128)(2,1)S(1)}, bf16[2048,256]{1,0:T(8,128)(2,1)}, u32[]{:S(2)}) copy-start(bf16[2048,256]{1,0:T(8,128)(2,1)} %param.11) | copy-start | bytes 3145732
  93.7 1.9 copy-start.1
  105.3 1.9 copy-start.1
  116.9 1.9 copy-start.1
  128.4 1.9 copy-start.1
  135.5 22.8 %all-to-all-start.1 = ((f32[128,1,16]{2,1,0:T(1,128)}), f32[128,1,16]{2,1,0:T(1,128)S(1)}, u32[]{:S(2)}, u32[]{:S(2)}) async-start(f32[128,1,16]{2,1,0:T(1,128)} %copy.18), calls=%async_computation.1 | async-start | bytes 131072 | tf_op jit(solution)/shard_map/all_to_all | solution.py:87
  158.3 18.1 %all-to-all-start.2 = ((f32[128,1,16]{2,1,0:T(1,128)}), f32[128,1,16]{2,1,0:T(1,128)S(1)}, u32[]{:S(2)}, u32[]{:S(2)}) async-start(f32[128,1,16]{2,1,0:T(1,128)} %copy.19), calls=%async_computation.2 | async-start | bytes 131072 | tf_op jit(solution)/shard_map/all_to_all | solution.py:88
  176.4 37.9 %all-to-all-start = ((f32[128,1,2048]{2,1,0:T(1,128)}), f32[128,1,2048]{2,1,0:T(1,128)S(1)}, u32[]{:S(2)}, u32[]{:S(2)}) async-start(f32[128,1,2048]{2,1,0:T(1,128)} %copy.17), calls=%async_computation | async-start | bytes 2097152 | tf_op jit(solution)/shard_map/all_to_all | solution.py:86
  181.1 195.3 %reduce-scatter.2.cloned.1.call-start = ((), (), s32[]{:S(2)}) async-start(), calls=%async_computation.4 | async-start | bytes 147456 | tf_op jit(solution)/shard_map/reduce_scatter | solution.py:103
Sparse Core Ops, SparseCore 0:
  295.1 81.2 reduce-scatter.1
where the time goes:
time: 386 us; the launch traced here: 385 us
  blocking collectives  159 us (41%)
  waiting for transfers between devices  139 us (36%)
  matrix products  21.2 us (5%)
  starting transfers between devices  18.6 us (5%)
  other arithmetic  16 us (4%)
  local copies, waits for them, and re-layouts  14.8 us (4%)
  between operations  13.5 us (3%)
    all_gather x1, blocking collectives, per_device(): all_queries = lax.all_gather(queries, 'ctx', axis=0, tiled=True)  81.4 us
    reduce_scatter x1, waiting for transfers between devices, per_device(): lax.psum_scatter(partial_out, 'kv', scatter_dimension=0, tiled=True)  81.4 us
    all_gather x1, blocking collectives, finish_rows(): lax.all_gather(attention_part, 'ctx', axis=0, tiled=True)  77.2 us
    all_to_all x1, waiting for transfers between devices, per_device(): lax.all_to_all(sent_out, 'ctx', split_axis=0, concat_axis=1, tiled=True)  32.9 us
    dot_general x4, matrix products, advance(): jnp.einsum('tkgs,skd->tkgd', weights.astype(jnp.bfloat16), value_block, p...  13.7 us
    all_to_all x1, waiting for transfers between devices, per_device(): lax.all_to_all(part_max, 'ctx', split_axis=0, concat_axis=1, tiled=True)  12.8 us
    all_to_all x1, waiting for transfers between devices, per_device(): lax.all_to_all(part_sum, 'ctx', split_axis=0, concat_axis=1, tiled=True)  11.6 us
    all_to_all x1, starting transfers between devices, per_device(): lax.all_to_all(part_max, 'ctx', split_axis=0, concat_axis=1, tiled=True)  9.28 us
  transfers between devices with their start and end apart: 4, of which 4 were waited for; matrix products, arithmetic and copies ran while one was open for 1% of the time, Pallas kernels for 0%

commit v1 on v0

v1 whole, which is shorter than its diff:
```python
import math

import jax
import jax.numpy as jnp
from jax import lax
from jax.experimental import pallas as pl
from jax.experimental.pallas import tpu as pltpu
from jax.sharding import Mesh
from jax.sharding import PartitionSpec as P

HD = 128
GROUP = 16
SCALE2 = math.log2(math.e) / math.sqrt(HD)
X, ZH, ZL = 4, 4, 4
OWNERS = X * ZL
STAT = 16
ROWS = HD + STAT
KEY_BLOCK = 256
HIDDEN = -1e30
LOWEST = -1e5

bf16 = jnp.bfloat16
f32 = jnp.float32
ROW_ROW = (((1,), (1,)), ((), ()))
ROW_COL = (((1,), (0,)), ((), ()))


def in_vmem(count):
    return [pl.BlockSpec(memory_space=pltpu.VMEM)] * count


def pack(out, top, total):
    high = total.astype(bf16).astype(f32)
    blank = jnp.zeros((STAT - 3, out.shape[1]), f32)
    return jnp.concatenate([out, top, high, total - high, blank], axis=0).astype(bf16)


def attend_kernel(info_ref, q_ref, k_ref, v_ref, o_ref, vt_ref, s_ref):
    keys = k_ref.shape[0]
    blocks = keys // KEY_BLOCK
    pairs = OWNERS // 2
    key_base, cached_end, span_start = info_ref[0], info_ref[1], info_ref[2]
    vt_ref[:HD, :] = v_ref[...].astype(f32).T.astype(bf16)
    vt_ref[HD:, :] = jnp.ones((STAT, keys), bf16)

    def query_rows(pair):
        parts = []
        for owner in (2 * pair, 2 * pair + 1):
            x, zl = owner // ZL, owner % ZL
            for zh in range(ZH):
                at = ((x * ZH + zh) * ZL + zl) * 2 * GROUP
                parts.append(q_ref[at : at + 2 * GROUP, :])
        return jnp.concatenate(parts, axis=0)

    def score(pair, masked):
        rows = query_rows(pair)
        top = None
        for block in range(blocks):
            span = slice(block * KEY_BLOCK, (block + 1) * KEY_BLOCK)
            s = lax.dot_general(k_ref[span, :], rows, ROW_ROW, preferred_element_type=f32)
            if masked:
                pos = key_base + block * KEY_BLOCK + lax.broadcasted_iota(jnp.int32, s.shape, 0)
                col = lax.broadcasted_iota(jnp.int32, s.shape, 1)
                owner = 2 * pair + (col >> 7)
                token = (
                    (owner >> 2) * 32 + ((col >> 5) & 3) * 8 + (owner & 3) * 2 + ((col >> 4) & 1)
                )
                visible = (pos < cached_end) | (pos >= span_start) & (pos <= span_start + token)
                s = jnp.where(visible, s, HIDDEN)
            s_ref[pair % 2, span, :] = s
            here = jnp.max(s.reshape(KEY_BLOCK // 8, 8, s.shape[1]), axis=0)
            top = here if top is None else jnp.maximum(top, here)
        top = jnp.max(top, axis=0, keepdims=True) * SCALE2
        return jnp.maximum(top, LOWEST).astype(bf16).astype(f32)

    def weigh(pair, top):
        total = None
        for block in range(blocks):
            span = slice(block * KEY_BLOCK, (block + 1) * KEY_BLOCK)
            w = jnp.exp2(s_ref[pair % 2, span, :] * SCALE2 - top).astype(bf16)
            part = lax.dot_general(vt_ref[:, span], w, ROW_COL, preferred_element_type=f32)
            total = part if total is None else total + part
        message = pack(total[:HD], top, total[HD : HD + 1])
        o_ref[2 * pair] = message[:, :HD]
        o_ref[2 * pair + 1] = message[:, HD:]

    def run(masked):
        top = score(0, masked)
        for pair in range(pairs):
            following = score(pair + 1, masked) if pair + 1 < pairs else None
            weigh(pair, top)
            top = following

    whole = key_base + keys <= cached_end
    pl.when(whole)(lambda: run(False))
    pl.when(jnp.logical_not(whole))(lambda: run(True))


def attend(info, queries, keys, values):
    count = keys.shape[0]
    return pl.pallas_call(
        attend_kernel,
        out_shape=jax.ShapeDtypeStruct((OWNERS, ROWS, HD), bf16),
        in_specs=[pl.BlockSpec(memory_space=pltpu.SMEM)] + in_vmem(3),
        out_specs=pl.BlockSpec(memory_space=pltpu.VMEM),
        scratch_shapes=[
            pltpu.VMEM((ROWS, count), bf16),
            pltpu.VMEM((2, count, 2 * HD), f32),
        ],
        compiler_params=pltpu.CompilerParams(vmem_limit_bytes=24 * 2**20),
        cost_estimate=pl.CostEstimate(
            flops=4 * queries.shape[0] * count * HD,
            bytes_accessed=2 * 2**20,
            transcendentals=queries.shape[0] * count,
        ),
        name="attend",
    )(info, queries, keys, values)


def merged(in_ref):
    senders = in_ref.shape[0]
    stats = [in_ref[i, HD:, :].astype(f32) for i in range(senders)]
    tops = [s[0:1] for s in stats]
    top = tops[0]
    for other in tops[1:]:
        top = jnp.maximum(top, other)
    out, total = None, None
    for i in range(senders):
        keep = jnp.exp2(tops[i] - top)
        part = in_ref[i, :HD, :].astype(f32) * keep
        part_sum = (stats[i][1:2] + stats[i][2:3]) * keep
        out = part if out is None else out + part
        total = part_sum if total is None else total + part_sum
    return out, top, total


def merge_kernel(in_ref, o_ref):
    message = pack(*merged(in_ref))
    for i in range(o_ref.shape[0]):
        o_ref[i] = message


def merge(came, copies):
    return pl.pallas_call(
        merge_kernel,
        out_shape=jax.ShapeDtypeStruct((copies, ROWS, HD), bf16),
        in_specs=in_vmem(1),
        out_specs=pl.BlockSpec(memory_space=pltpu.VMEM),
        name="merge",
    )(came)


def finish_kernel(in_ref, o_ref, turned_ref):
    out, _, total = merged(in_ref)
    turned_ref[...] = (out / total).T
    tokens = o_ref.shape[1]
    heads = [turned_ref[pl.ds(h, tokens, stride=GROUP), :] for h in range(GROUP)]
    rows = jnp.concatenate(heads, axis=1).astype(bf16)
    for i in range(o_ref.shape[0]):
        o_ref[i] = rows


def finish(came, copies):
    return pl.pallas_call(
        finish_kernel,
        out_shape=jax.ShapeDtypeStruct((copies, HD // GROUP, GROUP * HD), bf16),
        in_specs=in_vmem(1),
        out_specs=pl.BlockSpec(memory_space=pltpu.VMEM),
        scratch_shapes=[pltpu.VMEM((HD, HD), f32)],
        name="finish",
    )(came)


def project_kernel(a_ref, w_ref, o_ref):
    owners, tokens, depth = a_ref.shape
    rows = a_ref[...].astype(f32).reshape(owners * tokens, depth).astype(bf16)
    out = jnp.dot(rows, w_ref[...], preferred_element_type=f32)
    for x in range(X):
        for zh in range(ZH):
            for zl in range(ZL):
                at = ((x * ZL + zl) * ZH + zh) * 2
                to = (zh % 2) * 8 + zl * 2
                o_ref[x * 2 + zh // 2, to : to + 2, :] = out[at : at + 2]


def project(rows, weight):
    return pl.pallas_call(
        project_kernel,
        out_shape=jax.ShapeDtypeStruct((8, 16, weight.shape[1]), f32),
        in_specs=in_vmem(2),
        out_specs=pl.BlockSpec(memory_space=pltpu.VMEM),
        name="project",
    )(rows, weight)


def exchange(parts, axes):
    return lax.all_to_all(parts, axes, split_axis=0, concat_axis=0, tiled=True)


def spread(part, axes, count):
    return exchange(jnp.broadcast_to(part[None], (count,) + part.shape), axes)


def per_device(queries, cache_keys, cache_values, out_weight, cached_length, start):
    key_base = lax.axis_index(("x", "zh", "zl")) * cache_keys.shape[0]
    info = jnp.stack([key_base, cached_length[0], start[0]]).astype(jnp.int32)
    rows = queries.reshape(2 * GROUP, HD)
    rows = spread(rows, ("zh", "zl"), ZH * ZL)
    rows = spread(rows, ("x",), X)
    rows = rows.reshape(X * ZH * ZL * 2 * GROUP, HD)
    parts = attend(info, rows, cache_keys, cache_values)
    came = exchange(parts, ("x", "zl"))
    came = exchange(merge(came, ZH), ("zh",))
    attention = exchange(finish(came, OWNERS), ("x", "zl"))
    partial_out = exchange(project(attention, out_weight), ("y", "c"))
    return jnp.sum(partial_out, axis=0).astype(bf16)


def solution(mesh):
    fine = Mesh(mesh.devices.reshape(4, 2, X, ZH, ZL), ("y", "c", "x", "zh", "zl"))
    ctx, kv = ("x", "zh", "zl"), ("y", "c")
    return jax.shard_map(
        per_device,
        mesh=fine,
        in_specs=(P(ctx, kv), P(ctx, kv), P(ctx, kv), P(kv, ctx), P(), P()),
        out_specs=P(kv, ctx),
        check_vma=False,
    )
```

time: 386 us -> 124 us (0.32)
  waiting for transfers between devices: 139 us -> 5.56 us
  blocking collectives: 159 us -> 99 us
  matrix products: 21.2 us -> 0 us
  other arithmetic: 16 us -> 0.69 us
  starting transfers between devices: 18.6 us -> 4.14 us
  local copies, waits for them, and re-layouts: 14.8 us -> 1.6 us
  between operations: 13.5 us -> 1.32 us
  Pallas kernels: 0 us -> 10.8 us
    all_gather x2 -> x0, blocking collectives: 159 us -> none  [the longest x1 81.4 us: per_device(): all_queries = lax.all_gather(queries, 'ctx', axis=0, tiled=True)]
    all_to_all x0 -> x5, blocking collectives: none -> 99 us  [exchange(): return lax.all_to_all(parts, axes, split_axis=0, concat_axis=0, tiled=True)]
    reduce_scatter x1 -> x0, waiting for transfers between devices: 81.4 us -> none  [per_device(): lax.psum_scatter(partial_out, 'kv', scatter_dimension=0, tiled=True)]
    all_to_all x3 -> x1, waiting for transfers between devices: 57.3 us -> 5.56 us  [exchange(): return lax.all_to_all(parts, axes, split_axis=0, concat_axis=0, tiled=True)]
    dot_general x9 -> x0, matrix products: 21.2 us -> none  [the longest x4 13.7 us: advance(): jnp.einsum('tkgs,skd->tkgd', weights.astype(jnp.bfloat16), value_block, p...]
    all_to_all x3 -> x1, starting transfers between devices: 18.5 us -> 4.14 us  [exchange(): return lax.all_to_all(parts, axes, split_axis=0, concat_axis=0, tiled=True)]
    pallas_call x0 -> x4, Pallas kernels: none -> 10.8 us  [the longest x1 4.7 us: attend(): pl.pallas_call(attend_kernel, out_shape=jax.ShapeDtypeStruct((OWNERS, ROW...]
    while x14 -> x0, local copies, waits for them, and re-layouts: 9.12 us -> none
  transfers between devices with their start and end apart: 4 -> 1, of which waited for: 4 -> 1; matrix products, arithmetic and copies ran while one was open for 1% -> 0% of each run, Pallas kernels for 0% -> 0%
where the time goes in v1:
time: 124 us; the launch traced here: 123 us
  blocking collectives  99 us (80%)
  Pallas kernels  10.8 us (9%)
  waiting for transfers between devices  5.56 us (4%)
  starting transfers between devices  4.14 us (3%)
  local copies, waits for them, and re-layouts  1.6 us (1%)
  between operations  1.32 us (1%)
    all_to_all x5, blocking collectives, exchange(): return lax.all_to_all(parts, axes, split_axis=0, concat_axis=0, tiled=True)  99 us
    all_to_all x1, waiting for transfers between devices, exchange(): return lax.all_to_all(parts, axes, split_axis=0, concat_axis=0, tiled=True)  5.56 us
    pallas_call x1, Pallas kernels, attend(): pl.pallas_call(attend_kernel, out_shape=jax.ShapeDtypeStruct((OWNERS, ROW...  4.7 us
    all_to_all x1, starting transfers between devices, exchange(): return lax.all_to_all(parts, axes, split_axis=0, concat_axis=0, tiled=True)  4.14 us
  transfers between devices with their start and end apart: 1, of which 1 were waited for; matrix products, arithmetic and copies ran while one was open for 0% of the time, Pallas kernels for 0%

profile of v1, /device:TPU:1, one launch (start us, length us, event | category | flops | bytes accessed | tf_op | source)
XLA Modules:
  0.0 123.0 jit_solution(16348777782005671818)
XLA Ops:
  0.0 0.7 broadcast_in_dim.6
  0.7 27.5 %all_to_all.30 = bf16[16,32,128]{2,1,0:T(8,128)(2,1)S(1)} all-to-all(bf16[16,32,128]{2,1,0:T(8,128)(2,1)S(1)} %broadcast_in_dim.14), channel_id=1, replica_groups=mesh['y'=4,'c'=2,'x'=4,'zh'=4,'zl'=4] {'zh','zl'}, dimensions={0} | all-to-all | bytes 262144 | tf_op jit(solution)/shard_map/all_to_all | solution.py:197
  28.3 0.9 broadcast_in_dim.15
  29.1 0.0 copy-start
  29.1 0.0 copy-start.1
  29.1 4.1 %all-to-all-start.1 = ((bf16[4,16,32,128]{3,2,1,0:T(8,128)(2,1)}), bf16[4,16,32,128]{3,2,1,0:T(8,128)(2,1)S(1)}, u32[]{:S(2)}, u32[]{:S(2)}) async-start(bf16[4,16,32,128]{3,2,1,0:T(8,128)(2,1)} %broadcast_in_dim.15), calls=%async_computation.1 | async-start | bytes 1048576 | tf_op jit(solution)/shard_map/all_to_all | solution.py:197
  34.6 0.1 pad_add_fusion.info_ref
  34.7 5.6 %all-to-all-done.1 = bf16[4,16,32,128]{3,2,1,0:T(8,128)(2,1)S(1)} async-done(((bf16[4,16,32,128]{3,2,1,0:T(8,128)(2,1)}), bf16[4,16,32,128]{3,2,1,0:T(8,128)(2,1)S(1)}, u32[]{:S(2)}, u32[]{:S(2)}) %all-to-all-start.1) | async-done | bytes 524320 | tf_op jit(solution)/shard_map/all_to_all | solution.py:197
  40.2 0.0 copy-done
  40.2 0.0 copy-done.1
  40.2 4.7 %attend.1 = bf16[16,144,128]{2,1,0:T(8,128)(2,1)S(1)} custom-call(s32[3]{0:T(128)S(1)} %pad_add_fusion.info_ref, bf16[2048,128]{1,0:T(8,128)(2,1)S(1)} %bitcast.2, bf16[2048,128]{1,0:T(8,128)(2,1)S(1)} %copy-done, bf16[2048,128]{1,0:T(8,128)(2,1)S(1)} %copy-done.1), custom_call_target="tpu_custom_call" | custom-call | flops 2147483648 | bytes 2097152 | tf_op jit(solution)/shard_map/attend/pallas_call | solution.py:101
  44.9 21.4 %all_to_all.31.in_ref = bf16[16,144,128]{2,1,0:T(8,128)(2,1)} all-to-all(bf16[16,144,128]{2,1,0:T(8,128)(2,1)S(1)} %attend.1), channel_id=1, replica_groups=mesh['y'=4,'c'=2,'x'=4,'zh'=4,'zl'=4] {'x','zl'}, dimensions={0} | all-to-all | bytes 1179648 | tf_op jit(solution)/shard_map/all_to_all | solution.py:197
  66.3 1.9 %merge.1 = bf16[4,144,128]{2,1,0:T(8,128)(2,1)} custom-call(bf16[16,144,128]{2,1,0:T(8,128)(2,1)} %all_to_all.31.in_ref), custom_call_target="tpu_custom_call" | custom-call | tf_op jit(solution)/shard_map/merge/pallas_call | solution.py:144
  68.2 18.5 %all_to_all.32.in_ref = bf16[4,144,128]{2,1,0:T(8,128)(2,1)} all-to-all(bf16[4,144,128]{2,1,0:T(8,128)(2,1)} %merge.1), channel_id=1, replica_groups=mesh['y'=4,'c'=2,'x'=4,'zh'=4,'zl'=4] {'zh'}, dimensions={0} | all-to-all | bytes 294912 | tf_op jit(solution)/shard_map/all_to_all | solution.py:197
  86.6 1.9 %finish.1 = bf16[16,8,2048]{2,1,0:T(8,128)(2,1)} custom-call(bf16[4,144,128]{2,1,0:T(8,128)(2,1)} %all_to_all.32.in_ref), custom_call_target="tpu_custom_call" | custom-call | tf_op jit(solution)/shard_map/finish/pallas_call | solution.py:164
  88.5 16.1 %all_to_all.33.a_ref = bf16[16,8,2048]{2,1,0:T(8,128)(2,1)} all-to-all(bf16[16,8,2048]{2,1,0:T(8,128)(2,1)} %finish.1), channel_id=1, replica_groups=mesh['y'=4,'c'=2,'x'=4,'zh'=4,'zl'=4] {'x','zl'}, dimensions={0} | all-to-all | bytes 1048576 | tf_op jit(solution)/shard_map/all_to_all | solution.py:197
  104.7 2.3 %project.1 = f32[8,16,256]{2,1,0:T(8,128)} custom-call(bf16[16,8,2048]{2,1,0:T(8,128)(2,1)} %all_to_all.33.a_ref, bf16[2048,256]{1,0:T(8,128)(2,1)} %w_ref.1), custom_call_target="tpu_custom_call" | custom-call | tf_op jit(solution)/shard_map/project/pallas_call | solution.py:187
  107.0 15.4 %all_to_all.34 = f32[8,16,256]{2,1,0:T(8,128)S(1)} all-to-all(f32[8,16,256]{2,1,0:T(8,128)} %project.1), channel_id=1, replica_groups=mesh['y'=4,'c'=2,'x'=4,'zh'=4,'zl'=4] {'y','c'}, dimensions={0} | all-to-all | bytes 262144 | tf_op jit(solution)/shard_map/all_to_all | solution.py:197
  122.4 0.6 reduce_sum.9
  (1 shorter events, 0.0 us)
Async XLA Ops:
  29.1 11.1 %copy-start = (bf16[2048,128]{1,0:T(8,128)(2,1)S(1)}, bf16[2048,128]{1,0:T(8,128)(2,1)}, u32[]{:S(2)}) copy-start(bf16[2048,128]{1,0:T(8,128)(2,1)} %k_ref.1) | copy-start | bytes 1572868
  29.1 11.1 %copy-start.1 = (bf16[2048,128]{1,0:T(8,128)(2,1)S(1)}, bf16[2048,128]{1,0:T(8,128)(2,1)}, u32[]{:S(2)}) copy-start(bf16[2048,128]{1,0:T(8,128)(2,1)} %v_ref.1) | copy-start | bytes 1572868
  29.1 11.1 %all-to-all-start.1 = ((bf16[4,16,32,128]{3,2,1,0:T(8,128)(2,1)}), bf16[4,16,32,128]{3,2,1,0:T(8,128)(2,1)S(1)}, u32[]{:S(2)}, u32[]{:S(2)}) async-start(bf16[4,16,32,128]{3,2,1,0:T(8,128)(2,1)} %broadcast_in_dim.15), calls=%async_computation.1 | async-start | bytes 1048576 | tf_op jit(solution)/shard_map/all_to_all | solution.py:197

commit v2 on v1

v2 whole, which is shorter than its diff:
```python
import math

import jax
import jax.numpy as jnp
from jax import lax
from jax.experimental import pallas as pl
from jax.experimental.pallas import tpu as pltpu
from jax.sharding import Mesh
from jax.sharding import PartitionSpec as P

HD = 128
GROUP = 16
SCALE2 = math.log2(math.e) / math.sqrt(HD)
XA, XB, ZH, ZL = 2, 2, 4, 4
OWNERS = XA * XB * ZL
STAT = 16
ROWS = HD + STAT
KEY_BLOCK = 256
HIDDEN = -1e30
LOWEST = -1e5
MIB = 2**20

bf16 = jnp.bfloat16
f32 = jnp.float32
ROW_ROW = (((1,), (1,)), ((), ()))
ROW_COL = (((1,), (0,)), ((), ()))

def in_vmem(count):
    return [pl.BlockSpec(memory_space=pltpu.VMEM)] * count

def pack(out, top, total):
    high = total.astype(bf16).astype(f32)
    blank = jnp.zeros((STAT - 3, out.shape[1]), f32)
    return jnp.concatenate([out, top, high, total - high, blank], axis=0).astype(bf16)

def attend_kernel(info_ref, qa_ref, qb_ref, k_ref, v_ref, kv_ref, o_ref, vt_ref, s_ref, hide_ref):
    near = k_ref.shape[0]
    keys = 2 * near
    blocks = keys // KEY_BLOCK
    x, near_base, far_base, cached_end, span_start = [info_ref[i] for i in range(5)]
    xb = x & 1
    vt_ref[:HD, :near] = v_ref[...].astype(f32).T.astype(bf16)
    vt_ref[:HD, near:] = kv_ref[:, HD:].astype(f32).T.astype(bf16)
    vt_ref[HD:, :] = jnp.ones((STAT, keys), bf16)
    chunks = [(q, zl) for q in (0, 1) for zl in range(0, ZL, 2)]

    def query_rows(chunk):
        q, zl0 = chunk
        ref = (qa_ref, qb_ref)[q]
        parts = []
        for zl in (zl0, zl0 + 1):
            for zh in range(ZH):
                at = (zh * ZL + zl) * 2 * GROUP
                parts.append(ref[at : at + 2 * GROUP, :])
        return jnp.concatenate(parts, axis=0)

    def key_rows(block):
        at = block * KEY_BLOCK
        if at < near:
            return k_ref[at : at + KEY_BLOCK, :]
        return kv_ref[at - near : at - near + KEY_BLOCK, :HD]

    def hide():
        for half, base in ((0, near_base), (1, far_base)):
            pos = base + lax.broadcasted_iota(jnp.int32, (near, HD), 0)
            token = lax.broadcasted_iota(jnp.int32, (near, HD), 1)
            visible = (pos < cached_end) | (pos >= span_start) & (pos <= span_start + token)
            hide_ref[half * near : (half + 1) * near, :] = jnp.where(visible, 0.0, HIDDEN).astype(bf16)

    def token_rows(chunk):
        q, zl0 = chunk
        row = lax.broadcasted_iota(jnp.int32, (2 * HD, HD), 0)
        col = lax.broadcasted_iota(jnp.int32, (2 * HD, HD), 1)
        owner = x if q == 0 else x ^ 1
        token = owner * 32 + ((row >> 5) & 3) * 8 + (zl0 + (row >> 7)) * 2 + ((row >> 4) & 1)
        return jnp.where(token == col, 1.0, 0.0).astype(bf16)

    def score(i, masked):
        rows = query_rows(chunks[i])
        if masked:
            rows = jnp.concatenate([rows, token_rows(chunks[i])], axis=1)
        top = None
        for block in range(blocks):
            span = slice(block * KEY_BLOCK, (block + 1) * KEY_BLOCK)
            left = key_rows(block)
            if masked:
                left = jnp.concatenate([left, hide_ref[span, :]], axis=1)
            s = lax.dot_general(left, rows, ROW_ROW, preferred_element_type=f32)
            s_ref[i % 2, span, :] = s
            here = jnp.max(s.reshape(KEY_BLOCK // 8, 8, s.shape[1]), axis=0)
            top = here if top is None else jnp.maximum(top, here)
        top = jnp.max(top, axis=0, keepdims=True) * SCALE2
        return jnp.maximum(top, LOWEST).astype(bf16).astype(f32)

    def weigh(i, top):
        total = None
        for block in range(blocks):
            span = slice(block * KEY_BLOCK, (block + 1) * KEY_BLOCK)
            w = jnp.exp2(s_ref[i % 2, span, :] * SCALE2 - top).astype(bf16)
            part = lax.dot_general(vt_ref[:, span], w, ROW_COL, preferred_element_type=f32)
            total = part if total is None else total + part
        message = pack(total[:HD], top, total[HD : HD + 1])
        q, zl = chunks[i]
        to = (xb if q == 0 else 1 - xb) * ZL + zl
        o_ref[to] = message[:, :HD]
        o_ref[to + 1] = message[:, HD:]

    def run(masked):
        if masked:
            hide()
        top = score(0, masked)
        for i in range(len(chunks)):
            following = score(i + 1, masked) if i + 1 < len(chunks) else None
            weigh(i, top)
            top = following
    whole = (near_base + near <= cached_end) & (far_base + near <= cached_end)
    pl.when(whole)(lambda: run(False))
    pl.when(jnp.logical_not(whole))(lambda: run(True))

def attend(info, qa, qb, keys, values, far):
    count = 2 * keys.shape[0]
    return pl.pallas_call(
        attend_kernel,
        out_shape=jax.ShapeDtypeStruct((XB * ZL, ROWS, HD), bf16),
        in_specs=[pl.BlockSpec(memory_space=pltpu.SMEM)] + in_vmem(5),
        out_specs=pl.BlockSpec(memory_space=pltpu.VMEM),
        scratch_shapes=[
            pltpu.VMEM((ROWS, count), bf16),
            pltpu.VMEM((2, count, 2 * HD), f32),
            pltpu.VMEM((count, HD), bf16),
        ],
        compiler_params=pltpu.CompilerParams(vmem_limit_bytes=14 * MIB),
        name="attend",
    )(info, qa, qb, keys, values, far)

def merged(in_ref):
    senders = in_ref.shape[0]
    stats = [in_ref[i, HD:, :].astype(f32) for i in range(senders)]
    tops = [s[0:1] for s in stats]
    top = tops[0]
    for other in tops[1:]:
        top = jnp.maximum(top, other)
    out, total = None, None
    for i in range(senders):
        keep = jnp.exp2(tops[i] - top)
        part = in_ref[i, :HD, :].astype(f32) * keep
        part_sum = (stats[i][1:2] + stats[i][2:3]) * keep
        out = part if out is None else out + part
        total = part_sum if total is None else total + part_sum
    return out, top, total

def merge_kernel(in_ref, o_ref):
    message = pack(*merged(in_ref))
    for i in range(o_ref.shape[0]):
        o_ref[i] = message

def merge(came, copies):
    return pl.pallas_call(
        merge_kernel,
        out_shape=jax.ShapeDtypeStruct((copies, ROWS, HD), bf16),
        in_specs=in_vmem(1),
        out_specs=pl.BlockSpec(memory_space=pltpu.VMEM),
        compiler_params=pltpu.CompilerParams(vmem_limit_bytes=4 * MIB),
        name="merge",
    )(came)

def finish_kernel(in_ref, o_ref, turned_ref):
    out, _, total = merged(in_ref)
    turned_ref[...] = (out / total).T
    tokens = o_ref.shape[1]
    heads = [turned_ref[pl.ds(h, tokens, stride=GROUP), :] for h in range(GROUP)]
    rows = jnp.concatenate(heads, axis=1).astype(bf16)
    for i in range(o_ref.shape[0]):
        o_ref[i] = rows

def finish(came, copies):
    return pl.pallas_call(
        finish_kernel,
        out_shape=jax.ShapeDtypeStruct((copies, HD // GROUP, GROUP * HD), bf16),
        in_specs=in_vmem(1),
        out_specs=pl.BlockSpec(memory_space=pltpu.VMEM),
        scratch_shapes=[pltpu.VMEM((HD, HD), f32)],
        compiler_params=pltpu.CompilerParams(vmem_limit_bytes=4 * MIB),
        name="finish",
    )(came)

def project_kernel(a_ref, w_ref, o_ref):
    owners, tokens, depth = a_ref.shape
    rows = a_ref[...].astype(f32).reshape(owners * tokens, depth).astype(bf16)
    out = jnp.dot(rows, w_ref[...], preferred_element_type=f32)
    for x in range(4):
        for zh in range(ZH):
            for zl in range(ZL):
                at = ((x * ZL + zl) * ZH + zh) * 2
                to = (zh % 2) * 8 + zl * 2
                o_ref[x * 2 + zh // 2, to : to + 2, :] = out[at : at + 2]

def project(rows, weight):
    return pl.pallas_call(
        project_kernel,
        out_shape=jax.ShapeDtypeStruct((8, 16, weight.shape[1]), f32),
        in_specs=in_vmem(2),
        out_specs=pl.BlockSpec(memory_space=pltpu.VMEM),
        compiler_params=pltpu.CompilerParams(vmem_limit_bytes=8 * MIB),
        name="project",
    )(rows, weight)


def exchange(parts, axes):
    return lax.all_to_all(parts, axes, split_axis=0, concat_axis=0, tiled=True)


def spread(part, axes, count):
    return exchange(jnp.broadcast_to(part[None], (count,) + part.shape), axes)


def per_device(queries, cache_keys, cache_values, out_weight, cached_length, start):
    count = cache_keys.shape[0]
    x = lax.axis_index(("xa", "xb"))
    z = lax.axis_index(("zh", "zl"))
    depth = ZH * ZL
    near_base, far_base = (x * depth + z) * count, ((3 - x) * depth + z) * count
    info = jnp.stack([x, near_base, far_base, cached_length[0], start[0]]).astype(jnp.int32)
    cache = jnp.concatenate([cache_keys, cache_values], axis=1)
    cache, queries = lax.optimization_barrier((cache, queries))
    far = lax.ppermute(cache, ("xa", "xb"), [(0, 3), (3, 0), (1, 2), (2, 1)])
    own = spread(queries.reshape(2 * GROUP, HD), ("zh", "zl"), depth)
    own = own.reshape(depth * 2 * GROUP, HD)
    other = lax.ppermute(own, "xb", [(0, 1), (1, 0)])
    parts = attend(info, own, other, cache_keys, cache_values, far)
    came = exchange(parts, ("xb", "zl"))
    came = exchange(merge(came, ZH), ("zh",))
    attention = exchange(finish(came, OWNERS), ("xa", "xb", "zl"))
    partial_out = exchange(project(attention, out_weight), ("y", "c"))
    return jnp.sum(partial_out, axis=0).astype(bf16)


def solution(mesh):
    shape = (4, 2, XA, XB, ZH, ZL)
    fine = Mesh(mesh.devices.reshape(shape), ("y", "c", "xa", "xb", "zh", "zl"))
    ctx, kv = ("xa", "xb", "zh", "zl"), ("y", "c")
    return jax.shard_map(
        per_device,
        mesh=fine,
        in_specs=(P(ctx, kv), P(ctx, kv), P(ctx, kv), P(kv, ctx), P(), P()),
        out_specs=P(kv, ctx),
        check_vma=False,
    )
```

time: 124 us -> 108 us (0.87)
  blocking collectives: 99 us -> 88.6 us
  Pallas kernels: 10.8 us -> 5.59 us
  waiting for transfers between devices: 5.56 us -> 2.4 us
  starting transfers between devices: 4.14 us -> 7.13 us
  local copies, waits for them, and re-layouts: 1.6 us -> 0.13 us
  other arithmetic: 0.69 us -> 2.02 us
    all_to_all x5, blocking collectives: 99 us -> 88.6 us  [exchange(): return lax.all_to_all(parts, axes, split_axis=0, concat_axis=0, tiled=True)]
    ppermute x0 -> x2, starting transfers between devices: none -> 7.13 us  [the longest x1 5.22 us: per_device(): far = lax.ppermute(cache, ('xa', 'xb'), [(0, 3), (3, 0), (1, 2), (2, 1)])]
    all_to_all x1 -> x0, waiting for transfers between devices: 5.56 us -> none  [exchange(): return lax.all_to_all(parts, axes, split_axis=0, concat_axis=0, tiled=True)]
    all_to_all x1 -> x0, starting transfers between devices: 4.14 us -> none  [exchange(): return lax.all_to_all(parts, axes, split_axis=0, concat_axis=0, tiled=True)]
    ppermute x0 -> x2, waiting for transfers between devices: none -> 2.4 us  [the longest x1 2.39 us: per_device(): other = lax.ppermute(own, 'xb', [(0, 1), (1, 0)])]
    pallas_call x1, Pallas kernels: 2.34 us -> 0.31 us  [project(): pl.pallas_call(project_kernel, out_shape=jax.ShapeDtypeStruct((8, 16, wei...]
    pallas_call x1, Pallas kernels: 1.87 us -> 0.08 us  [merge(): pl.pallas_call(merge_kernel, out_shape=jax.ShapeDtypeStruct((copies, ROWS...]
    pallas_call x1, Pallas kernels: 1.87 us -> 0.18 us  [finish(): pl.pallas_call(finish_kernel, out_shape=jax.ShapeDtypeStruct((copies, HD...]
  transfers between devices with their start and end apart: 1 -> 2, of which waited for: 1 -> 1; matrix products, arithmetic and copies ran while one was open for 0% -> 0% of each run, Pallas kernels for 0% -> 0%
where the time goes in v2:
time: 108 us; the launch traced here: 107 us
  blocking collectives  88.6 us (82%)
  starting transfers between devices  7.13 us (7%)
  Pallas kernels  5.59 us (5%)
  waiting for transfers between devices  2.4 us (2%)
  other arithmetic  2.02 us (2%)
  between operations  1.39 us (1%)
    all_to_all x5, blocking collectives, exchange(): return lax.all_to_all(parts, axes, split_axis=0, concat_axis=0, tiled=True)  88.6 us
    ppermute x1, starting transfers between devices, per_device(): far = lax.ppermute(cache, ('xa', 'xb'), [(0, 3), (3, 0), (1, 2), (2, 1)])  5.22 us
    pallas_call x1, Pallas kernels, attend(): pl.pallas_call(attend_kernel, out_shape=jax.ShapeDtypeStruct((XB * ZL, RO...  5.02 us
    ppermute x1, waiting for transfers between devices, per_device(): other = lax.ppermute(own, 'xb', [(0, 1), (1, 0)])  2.39 us
  transfers between devices with their start and end apart: 2, of which 1 were waited for; matrix products, arithmetic and copies ran while one was open for 0% of the time, Pallas kernels for 0%

profile of v2, /device:TPU:1, one launch (start us, length us, event | category | flops | bytes accessed | tf_op | source)
XLA Modules:
  0.0 107.3 jit_solution(3819928046127710909)
XLA Ops:
  0.0 0.0 copy-start.1
  0.0 0.0 copy-start
  0.0 0.0 copy-start.3
  0.0 1.4 %pad_maximum_fusion = bf16[2048,256]{1,0:T(8,128)(2,1)S(1)} fusion(bf16[2048,128]{1,0:T(8,128)(2,1)} %v_ref.1, bf16[2048,128]{1,0:T(8,128)(2,1)} %k_ref.1), kind=kLoop, calls=%fused_computation | loop fusion | flops 2097152 | bytes 2097152 | tf_op jit(solution)/shard_map/concatenate | solution.py:224
  1.4 5.2 %collective-permute-start.1 = (bf16[2048,256]{1,0:T(8,128)(2,1)S(1)}, bf16[2048,256]{1,0:T(8,128)(2,1)S(1)}, u32[]{:S(2)}, u32[]{:S(2)}) collective-permute-start(bf16[2048,256]{1,0:T(8,128)(2,1)S(1)} %pad_maximum_fusion), channel_id=1, source_target_pairs={{0,48},{48,0},{16,32},{32,16},{1,49},{49,1},{17,33},{33,17},{2,50}... | collective-permute-start | bytes 3145736 | tf_op jit(solution)/shard_map/ppermute | solution.py:226
  6.6 0.0 copy-done.3
  6.7 26.7 %all_to_all.25 = bf16[16,32,128]{2,1,0:T(8,128)(2,1)S(1)} all-to-all(bf16[16,32,128]{2,1,0:T(8,128)(2,1)S(1)} %broadcast_in_dim.8), channel_id=1, replica_groups=mesh['y'=4,'c'=2,'xa'=2,'xb'=2,'zh'=4,'zl'=4] {'zh','zl'}, dimensions={0} | all-to-all | bytes 262144 | tf_op jit(solution)/shard_map/all_to_all | solution.py:210
  33.4 1.9 %collective-permute-start = (bf16[512,128]{1,0:T(8,128)(2,1)S(1)}, bf16[512,128]{1,0:T(8,128)(2,1)S(1)}, u32[]{:S(2)}, u32[]{:S(2)}) collective-permute-start(bf16[512,128]{1,0:T(8,128)(2,1)S(1)} %bitcast.4), channel_id=1, source_target_pairs={{0,16},{16,0},{1,17},{17,1},{2,18},{18,2},{3,19},{19,3},{4,20},{20... | collective-permute-start | bytes 393224 | tf_op jit(solution)/shard_map/ppermute | solution.py:229
  36.6 0.1 stack.15.info_ref
  36.7 2.4 %collective-permute-done.qb_ref = bf16[512,128]{1,0:T(8,128)(2,1)S(1)} collective-permute-done((bf16[512,128]{1,0:T(8,128)(2,1)S(1)}, bf16[512,128]{1,0:T(8,128)(2,1)S(1)}, u32[]{:S(2)}, u32[]{:S(2)}) %collective-permute-start) | collective-permute-done | bytes 131104 | tf_op jit(solution)/shard_map/ppermute | solution.py:229
  39.1 0.0 collective-permute-done.1.kv_ref
  39.1 0.0 copy-done.1
  39.1 0.0 copy-done
  39.1 5.0 %attend.1 = bf16[8,144,128]{2,1,0:T(8,128)(2,1)S(1)} custom-call(s32[5]{0:T(128)S(1)} %stack.15.info_ref, bf16[512,128]{1,0:T(8,128)(2,1)S(1)} %bitcast.5, bf16[512,128]{1,0:T(8,128)(2,1)S(1)} %collective-permute-done.qb_ref, bf16[2048,128]{1,0:T(8,128)(2,1)S(1)} %copy-done, bf16[2048,128]{1,0:T(8,128)(2,1)S(1)} %copy-done.1, ...), custom_call_target="tpu_custom_call" | custom-call | tf_op jit(solution)/shard_map/attend/pallas_call | solution.py:122
  44.1 11.4 %all_to_all.26.in_ref = bf16[8,144,128]{2,1,0:T(8,128)(2,1)S(1)} all-to-all(bf16[8,144,128]{2,1,0:T(8,128)(2,1)S(1)} %attend.1), channel_id=1, replica_groups=mesh['y'=4,'c'=2,'xa'=2,'xb'=2,'zh'=4,'zl'=4] {'xb','zl'}, dimensions={0} | all-to-all | bytes 589824 | tf_op jit(solution)/shard_map/all_to_all | solution.py:210
  55.6 0.1 merge.1
  55.7 0.0 copy-start.2
  55.7 18.3 %all_to_all.27.in_ref = bf16[4,144,128]{2,1,0:T(8,128)(2,1)S(1)} all-to-all(bf16[4,144,128]{2,1,0:T(8,128)(2,1)S(1)} %merge.1), channel_id=1, replica_groups=mesh['y'=4,'c'=2,'xa'=2,'xb'=2,'zh'=4,'zl'=4] {'zh'}, dimensions={0} | all-to-all | bytes 294912 | tf_op jit(solution)/shard_map/all_to_all | solution.py:210
  74.0 0.2 finish.1
  74.2 16.5 %all_to_all.28.a_ref = bf16[16,8,2048]{2,1,0:T(8,128)(2,1)S(1)} all-to-all(bf16[16,8,2048]{2,1,0:T(8,128)(2,1)S(1)} %finish.1), channel_id=1, replica_groups=mesh['y'=4,'c'=2,'xa'=2,'xb'=2,'zh'=4,'zl'=4] {'xa','xb','zl'}, dimensions={0} | all-to-all | bytes 1048576 | tf_op jit(solution)/shard_map/all_to_all | solution.py:210
  90.7 0.0 copy-done.2
  90.7 0.3 project.1
  91.0 15.7 %all_to_all.29 = f32[8,16,256]{2,1,0:T(8,128)S(1)} all-to-all(f32[8,16,256]{2,1,0:T(8,128)S(1)} %project.1), channel_id=1, replica_groups=mesh['y'=4,'c'=2,'xa'=2,'xb'=2,'zh'=4,'zl'=4] {'y','c'}, dimensions={0} | all-to-all | bytes 262144 | tf_op jit(solution)/shard_map/all_to_all | solution.py:210
  106.7 0.6 reduce_sum.9
  (2 shorter events, 0.0 us)
Async XLA Ops:
  0.0 39.1 %copy-start.1 = (bf16[2048,128]{1,0:T(8,128)(2,1)S(1)}, bf16[2048,128]{1,0:T(8,128)(2,1)}, u32[]{:S(2)}) copy-start(bf16[2048,128]{1,0:T(8,128)(2,1)} %v_ref.1) | copy-start | bytes 1572868
  0.0 39.1 %copy-start = (bf16[2048,128]{1,0:T(8,128)(2,1)S(1)}, bf16[2048,128]{1,0:T(8,128)(2,1)}, u32[]{:S(2)}) copy-start(bf16[2048,128]{1,0:T(8,128)(2,1)} %k_ref.1) | copy-start | bytes 1572868
  0.0 6.6 %copy-start.3 = (bf16[2,2048]{1,0:T(2,128)(2,1)S(1)}, bf16[2,2048]{1,0:T(2,128)(2,1)}, u32[]{:S(2)}) copy-start(bf16[2,2048]{1,0:T(2,128)(2,1)} %param.6) | copy-start | bytes 24580
  1.4 37.7 %collective-permute-start.1 = (bf16[2048,256]{1,0:T(8,128)(2,1)S(1)}, bf16[2048,256]{1,0:T(8,128)(2,1)S(1)}, u32[]{:S(2)}, u32[]{:S(2)}) collective-permute-start(bf16[2048,256]{1,0:T(8,128)(2,1)S(1)} %pad_maximum_fusion), channel_id=1, source_target_pairs={{0,48},{48,0},{16,32},{32,16},{1,49},{49,1},{17,33},{33,17},{2,50}... | collective-permute-start | bytes 3145736 | tf_op jit(solution)/shard_map/ppermute | solution.py:226
  33.4 5.7 %collective-permute-start = (bf16[512,128]{1,0:T(8,128)(2,1)S(1)}, bf16[512,128]{1,0:T(8,128)(2,1)S(1)}, u32[]{:S(2)}, u32[]{:S(2)}) collective-permute-start(bf16[512,128]{1,0:T(8,128)(2,1)S(1)} %bitcast.4), channel_id=1, source_target_pairs={{0,16},{16,0},{1,17},{17,1},{2,18},{18,2},{3,19},{19,3},{4,20},{20... | collective-permute-start | bytes 393224 | tf_op jit(solution)/shard_map/ppermute | solution.py:229
  55.7 35.0 %copy-start.2 = (bf16[2048,256]{1,0:T(8,128)(2,1)S(1)}, bf16[2048,256]{1,0:T(8,128)(2,1)}, u32[]{:S(2)}) copy-start(bf16[2048,256]{1,0:T(8,128)(2,1)} %w_ref.1) | copy-start | bytes 3145732

commit v3 on v2

--- a/solution.py
+++ b/solution.py
@@ -1,3 +1,4 @@
+import functools
 import math
 
 import jax
@@ -33,52 +34,48 @@
     blank = jnp.zeros((STAT - 3, out.shape[1]), f32)
     return jnp.concatenate([out, top, high, total - high, blank], axis=0).astype(bf16)
 
-def attend_kernel(info_ref, qa_ref, qb_ref, k_ref, v_ref, kv_ref, o_ref, vt_ref, s_ref, hide_ref):
+def attend_kernel(info_ref, q_ref, k_ref, v_ref, far_ref, *refs, own):
+    if own:
+        o_ref, vt_ref, hide_ref, s_ref = refs
+    else:
+        vt_ref, hide_ref, _, o_ref, s_ref = refs
     near = k_ref.shape[0]
-    keys = 2 * near
-    blocks = keys // KEY_BLOCK
+    blocks = 2 * near // KEY_BLOCK
     x, near_base, far_base, cached_end, span_start = [info_ref[i] for i in range(5)]
-    xb = x & 1
-    vt_ref[:HD, :near] = v_ref[...].astype(f32).T.astype(bf16)
-    vt_ref[:HD, near:] = kv_ref[:, HD:].astype(f32).T.astype(bf16)
-    vt_ref[HD:, :] = jnp.ones((STAT, keys), bf16)
-    chunks = [(q, zl) for q in (0, 1) for zl in range(0, ZL, 2)]
-
-    def query_rows(chunk):
-        q, zl0 = chunk
-        ref = (qa_ref, qb_ref)[q]
+    owner = x if own else x ^ 1
+
+    def query_rows(zl0):
         parts = []
         for zl in (zl0, zl0 + 1):
             for zh in range(ZH):
                 at = (zh * ZL + zl) * 2 * GROUP
-                parts.append(ref[at : at + 2 * GROUP, :])
+                parts.append(q_ref[at : at + 2 * GROUP, :])
         return jnp.concatenate(parts, axis=0)
 
     def key_rows(block):
         at = block * KEY_BLOCK
         if at < near:
             return k_ref[at : at + KEY_BLOCK, :]
-        return kv_ref[at - near : at - near + KEY_BLOCK, :HD]
+        return far_ref[at - near : at - near + KEY_BLOCK, :HD]
 
     def hide():
         for half, base in ((0, near_base), (1, far_base)):
             pos = base + lax.broadcasted_iota(jnp.int32, (near, HD), 0)
             token = lax.broadcasted_iota(jnp.int32, (near, HD), 1)
             visible = (pos < cached_end) | (pos >= span_start) & (pos <= span_start + token)
-            hide_ref[half * near : (half + 1) * near, :] = jnp.where(visible, 0.0, HIDDEN).astype(bf16)
-
-    def token_rows(chunk):
-        q, zl0 = chunk
+            hidden = jnp.where(visible, 0.0, HIDDEN)
+            hide_ref[half * near : (half + 1) * near, :] = hidden.astype(bf16)
+
+    def token_rows(zl0):
         row = lax.broadcasted_iota(jnp.int32, (2 * HD, HD), 0)
         col = lax.broadcasted_iota(jnp.int32, (2 * HD, HD), 1)
-        owner = x if q == 0 else x ^ 1
-        token = owner * 32 + ((row >> 5) & 3) * 8 + (zl0 + (row >> 7)) * 2 + ((row >> 4) & 1)
-        return jnp.where(token == col, 1.0, 0.0).astype(bf16)
-
-    def score(i, masked):
-        rows = query_rows(chunks[i])
+        zh, zl, t = (row >> 5) & 3, zl0 + (row >> 7), (row >> 4) & 1
+        return jnp.where(owner * 32 + zh * 8 + zl * 2 + t == col, 1.0, 0.0).astype(bf16)
+
+    def score(zl0, slot, masked):
+        rows = query_rows(zl0)
         if masked:
-            rows = jnp.concatenate([rows, token_rows(chunks[i])], axis=1)
+            rows = jnp.concatenate([rows, token_rows(zl0)], axis=1)
         top = None
         for block in range(blocks):
             span = slice(block * KEY_BLOCK, (block + 1) * KEY_BLOCK)
@@ -86,52 +83,67 @@
             if masked:
                 left = jnp.concatenate([left, hide_ref[span, :]], axis=1)
             s = lax.dot_general(left, rows, ROW_ROW, preferred_element_type=f32)
-            s_ref[i % 2, span, :] = s
+            s_ref[slot, span, :] = s
             here = jnp.max(s.reshape(KEY_BLOCK // 8, 8, s.shape[1]), axis=0)
             top = here if top is None else jnp.maximum(top, here)
         top = jnp.max(top, axis=0, keepdims=True) * SCALE2
         return jnp.maximum(top, LOWEST).astype(bf16).astype(f32)
 
-    def weigh(i, top):
+    def weigh(zl0, slot, top):
         total = None
         for block in range(blocks):
             span = slice(block * KEY_BLOCK, (block + 1) * KEY_BLOCK)
-            w = jnp.exp2(s_ref[i % 2, span, :] * SCALE2 - top).astype(bf16)
+            w = jnp.exp2(s_ref[slot, span, :] * SCALE2 - top).astype(bf16)
             part = lax.dot_general(vt_ref[:, span], w, ROW_COL, preferred_element_type=f32)
             total = part if total is None else total + part
         message = pack(total[:HD], top, total[HD : HD + 1])
-        q, zl = chunks[i]
-        to = (xb if q == 0 else 1 - xb) * ZL + zl
+        to = (owner & 1) * ZL + zl0
         o_ref[to] = message[:, :HD]
         o_ref[to + 1] = message[:, HD:]
 
     def run(masked):
-        if masked:
+        if own and masked:
             hide()
-        top = score(0, masked)
-        for i in range(len(chunks)):
-            following = score(i + 1, masked) if i + 1 < len(chunks) else None
-            weigh(i, top)
-            top = following
+        first = score(0, 0, masked)
+        if own:
+            vt_ref[:HD, :near] = v_ref[...].astype(f32).T.astype(bf16)
+            vt_ref[:HD, near:] = far_ref[:, HD:].astype(f32).T.astype(bf16)
+            vt_ref[HD:, :] = jnp.ones((STAT, 2 * near), bf16)
+        second = score(2, 1, masked)
+        weigh(0, 0, first)
+        weigh(2, 1, second)
+
     whole = (near_base + near <= cached_end) & (far_base + near <= cached_end)
     pl.when(whole)(lambda: run(False))
     pl.when(jnp.logical_not(whole))(lambda: run(True))
 
-def attend(info, qa, qb, keys, values, far):
+
+def attend(info, queries, keys, values, far, earlier=None):
+    own = earlier is None
     count = 2 * keys.shape[0]
-    return pl.pallas_call(
-        attend_kernel,
-        out_shape=jax.ShapeDtypeStruct((XB * ZL, ROWS, HD), bf16),
-        in_specs=[pl.BlockSpec(memory_space=pltpu.SMEM)] + in_vmem(5),
-        out_specs=pl.BlockSpec(memory_space=pltpu.VMEM),
-        scratch_shapes=[
-            pltpu.VMEM((ROWS, count), bf16),
-            pltpu.VMEM((2, count, 2 * HD), f32),
-            pltpu.VMEM((count, HD), bf16),
-        ],
+    message = jax.ShapeDtypeStruct((XB * ZL, ROWS, HD), bf16)
+    turned = jax.ShapeDtypeStruct((ROWS, count), bf16)
+    hidden = jax.ShapeDtypeStruct((count, HD), bf16)
+    operands = [info, queries, keys, values, far]
+    if not own:
+        parts, turned_values, mask = earlier
+        operands += [turned_values, mask, parts]
+    return pl.pallas_call(
+        functools.partial(attend_kernel, own=own),
+        out_shape=(message, turned, hidden) if own else message,
+        in_specs=[pl.BlockSpec(memory_space=pltpu.SMEM)] + in_vmem(len(operands) - 1),
+        out_specs=tuple(in_vmem(3)) if own else in_vmem(1)[0],
+        scratch_shapes=[pltpu.VMEM((2, count, 2 * HD), f32)],
+        input_output_aliases={} if own else {7: 0},
         compiler_params=pltpu.CompilerParams(vmem_limit_bytes=14 * MIB),
-        name="attend",
-    )(info, qa, qb, keys, values, far)
+        cost_estimate=pl.CostEstimate(
+            flops=4 * queries.shape[0] * count * HD,
+            bytes_accessed=4 * MIB,
+            transcendentals=queries.shape[0] * count,
+        ),
+        name="attend_own" if own else "attend_other",
+    )(*operands)
+
 
 def merged(in_ref):
     senders = in_ref.shape[0]
@@ -227,7 +239,8 @@
     own = spread(queries.reshape(2 * GROUP, HD), ("zh", "zl"), depth)
     own = own.reshape(depth * 2 * GROUP, HD)
     other = lax.ppermute(own, "xb", [(0, 1), (1, 0)])
-    parts = attend(info, own, other, cache_keys, cache_values, far)
+    earlier = attend(info, own, cache_keys, cache_values, far)
+    parts = attend(info, other, cache_keys, cache_values, far, earlier)
     came = exchange(parts, ("xb", "zl"))
     came = exchange(merge(came, ZH), ("zh",))
     attention = exchange(finish(came, OWNERS), ("xa", "xb", "zl"))

time: 108 us -> 109 us (level)
  blocking collectives: 88.6 us -> 91.2 us
  waiting for transfers between devices: 2.4 us -> 0.01 us
  Pallas kernels: 5.59 us -> 6.74 us
    all_to_all x5, blocking collectives: 88.6 us -> 91.2 us  [exchange(): return lax.all_to_all(parts, axes, split_axis=0, concat_axis=0, tiled=True)]
    ppermute x1, waiting for transfers between devices: 2.39 us -> 0.01 us  [per_device(): other = lax.ppermute(own, 'xb', [(0, 1), (1, 0)])]
    pallas_call x1 -> x2, Pallas kernels: 5.02 us -> 6.16 us  [attend(): pl.pallas_call(functools.partial(attend_kernel, own=own), out_shape=(mess...]
  transfers between devices with their start and end apart: 2 -> 2, of which waited for: 1 -> 0; matrix products, arithmetic and copies ran while one was open for 0% -> 0% of each run, Pallas kernels for 0% -> 3%
where the time goes in v3:
time: 109 us
  blocking collectives  91.2 us (84%)
  starting transfers between devices  7.13 us (7%)
  Pallas kernels  6.74 us (6%)
  other arithmetic  2.02 us (2%)
  between operations  1.4 us (1%)
    all_to_all x5, blocking collectives, exchange(): return lax.all_to_all(parts, axes, split_axis=0, concat_axis=0, tiled=True)  91.2 us
    pallas_call x2, Pallas kernels, attend(): pl.pallas_call(functools.partial(attend_kernel, own=own), out_shape=(mess...  6.16 us
    ppermute x1, starting transfers between devices, per_device(): far = lax.ppermute(cache, ('xa', 'xb'), [(0, 3), (3, 0), (1, 2), (2, 1)])  5.22 us
  transfers between devices with their start and end apart: 2, of which 0 were waited for; matrix products, arithmetic and copies ran while one was open for 0% of the time, Pallas kernels for 3%

profile of v3, /device:TPU:1, one launch (start us, length us, event | category | flops | bytes accessed | tf_op | source)
XLA Modules:
  0.0 108.6 jit_solution(6423547087782648433)
XLA Ops:
  0.0 0.0 copy-start.1
  0.0 0.0 copy-start
  0.0 0.0 copy-start.3
  0.0 1.4 %pad_maximum_fusion = bf16[2048,256]{1,0:T(8,128)(2,1)S(1)} fusion(bf16[2048,128]{1,0:T(8,128)(2,1)} %v_ref.3, bf16[2048,128]{1,0:T(8,128)(2,1)} %k_ref.3), kind=kLoop, calls=%fused_computation | loop fusion | flops 2097152 | bytes 2097152 | tf_op jit(solution)/shard_map/concatenate | solution.py:236
  1.4 5.2 %collective-permute-start.1 = (bf16[2048,256]{1,0:T(8,128)(2,1)S(1)}, bf16[2048,256]{1,0:T(8,128)(2,1)S(1)}, u32[]{:S(2)}, u32[]{:S(2)}) collective-permute-start(bf16[2048,256]{1,0:T(8,128)(2,1)S(1)} %pad_maximum_fusion), channel_id=1, source_target_pairs={{0,48},{48,0},{16,32},{32,16},{1,49},{49,1},{17,33},{33,17},{2,50}... | collective-permute-start | bytes 3145736 | tf_op jit(solution)/shard_map/ppermute | solution.py:238
  6.6 0.0 copy-done.3
  6.7 26.7 %all_to_all.25 = bf16[16,32,128]{2,1,0:T(8,128)(2,1)S(1)} all-to-all(bf16[16,32,128]{2,1,0:T(8,128)(2,1)S(1)} %broadcast_in_dim.8), channel_id=1, replica_groups=mesh['y'=4,'c'=2,'xa'=2,'xb'=2,'zh'=4,'zl'=4] {'zh','zl'}, dimensions={0} | all-to-all | bytes 262144 | tf_op jit(solution)/shard_map/all_to_all | solution.py:222
  33.4 1.9 %collective-permute-start = (bf16[512,128]{1,0:T(8,128)(2,1)S(1)}, bf16[512,128]{1,0:T(8,128)(2,1)S(1)}, u32[]{:S(2)}, u32[]{:S(2)}) collective-permute-start(bf16[512,128]{1,0:T(8,128)(2,1)S(1)} %bitcast.4), channel_id=1, source_target_pairs={{0,16},{16,0},{1,17},{17,1},{2,18},{18,2},{3,19},{19,3},{4,20},{20... | collective-permute-start | bytes 393224 | tf_op jit(solution)/shard_map/ppermute | solution.py:241
  36.6 0.1 stack.15.info_ref
  36.7 0.0 collective-permute-done.1.far_ref
  36.7 0.0 copy-done.1
  36.7 0.0 copy-done
  36.7 3.2 %attend_own.1 = (bf16[8,144,128]{2,1,0:T(8,128)(2,1)S(1)}, bf16[144,4096]{1,0:T(8,128)(2,1)S(1)}, bf16[4096,128]{1,0:T(8,128)(2,1)S(1)}) custom-call(s32[5]{0:T(128)S(1)} %stack.15.info_ref, bf16[512,128]{1,0:T(8,128)(2,1)S(1)} %bitcast.5, bf16[2048,128]{1,0:T(8,128)(2,1)S(1)} %copy-done, bf16[2048,128]{1,0:T(8,128)(2,1)S(1)} %copy-done.1, ...), custom_call_target="tpu_custom_call" | custom-call | flops 1073741824 | bytes 4194304 | tf_op jit(solution)/shard_map/attend_own/pallas_call | solution.py:131
  39.9 0.0 collective-permute-done.q_ref
  39.9 3.0 %attend_other.1 = bf16[8,144,128]{2,1,0:T(8,128)(2,1)S(1)} custom-call(s32[5]{0:T(128)S(1)} %stack.15.info_ref, bf16[512,128]{1,0:T(8,128)(2,1)S(1)} %collective-permute-done.q_ref, bf16[2048,128]{1,0:T(8,128)(2,1)S(1)} %copy-done, bf16[2048,128]{1,0:T(8,128)(2,1)S(1)} %copy-done.1, ...), custom_call_target="tpu_custom_call", output_to_operand_aliasing={{}: (7, {})} | custom-call | flops 1073741824 | bytes 4194304 | tf_op jit(solution)/shard_map/attend_other/pallas_call | solution.py:131
  42.9 12.6 %all_to_all.26.in_ref = bf16[8,144,128]{2,1,0:T(8,128)(2,1)S(1)} all-to-all(bf16[8,144,128]{2,1,0:T(8,128)(2,1)S(1)} %attend_other.1), channel_id=1, replica_groups=mesh['y'=4,'c'=2,'xa'=2,'xb'=2,'zh'=4,'zl'=4] {'xb','zl'}, dimensions={0} | all-to-all | bytes 589824 | tf_op jit(solution)/shard_map/all_to_all | solution.py:222
  55.5 0.0 copy-start.2
  55.5 0.1 merge.1
  55.6 19.1 %all_to_all.27.in_ref = bf16[4,144,128]{2,1,0:T(8,128)(2,1)S(1)} all-to-all(bf16[4,144,128]{2,1,0:T(8,128)(2,1)S(1)} %merge.1), channel_id=1, replica_groups=mesh['y'=4,'c'=2,'xa'=2,'xb'=2,'zh'=4,'zl'=4] {'zh'}, dimensions={0} | all-to-all | bytes 294912 | tf_op jit(solution)/shard_map/all_to_all | solution.py:222
  74.7 0.2 finish.1
  74.9 17.0 %all_to_all.28.a_ref = bf16[16,8,2048]{2,1,0:T(8,128)(2,1)S(1)} all-to-all(bf16[16,8,2048]{2,1,0:T(8,128)(2,1)S(1)} %finish.1), channel_id=1, replica_groups=mesh['y'=4,'c'=2,'xa'=2,'xb'=2,'zh'=4,'zl'=4] {'xa','xb','zl'}, dimensions={0} | all-to-all | bytes 1048576 | tf_op jit(solution)/shard_map/all_to_all | solution.py:222
  91.9 0.0 copy-done.2
  92.0 0.3 project.1
  92.3 15.7 %all_to_all.29 = f32[8,16,256]{2,1,0:T(8,128)S(1)} all-to-all(f32[8,16,256]{2,1,0:T(8,128)S(1)} %project.1), channel_id=1, replica_groups=mesh['y'=4,'c'=2,'xa'=2,'xb'=2,'zh'=4,'zl'=4] {'y','c'}, dimensions={0} | all-to-all | bytes 262144 | tf_op jit(solution)/shard_map/all_to_all | solution.py:222
  108.0 0.6 reduce_sum.9
  (2 shorter events, 0.0 us)
Async XLA Ops:
  0.0 36.7 %copy-start.1 = (bf16[2048,128]{1,0:T(8,128)(2,1)S(1)}, bf16[2048,128]{1,0:T(8,128)(2,1)}, u32[]{:S(2)}) copy-start(bf16[2048,128]{1,0:T(8,128)(2,1)} %v_ref.3) | copy-start | bytes 1572868
  0.0 36.7 %copy-start = (bf16[2048,128]{1,0:T(8,128)(2,1)S(1)}, bf16[2048,128]{1,0:T(8,128)(2,1)}, u32[]{:S(2)}) copy-start(bf16[2048,128]{1,0:T(8,128)(2,1)} %k_ref.3) | copy-start | bytes 1572868
  0.0 6.6 %copy-start.3 = (bf16[2,2048]{1,0:T(2,128)(2,1)S(1)}, bf16[2,2048]{1,0:T(2,128)(2,1)}, u32[]{:S(2)}) copy-start(bf16[2,2048]{1,0:T(2,128)(2,1)} %param.6) | copy-start | bytes 24580
  1.4 35.3 %collective-permute-start.1 = (bf16[2048,256]{1,0:T(8,128)(2,1)S(1)}, bf16[2048,256]{1,0:T(8,128)(2,1)S(1)}, u32[]{:S(2)}, u32[]{:S(2)}) collective-permute-start(bf16[2048,256]{1,0:T(8,128)(2,1)S(1)} %pad_maximum_fusion), channel_id=1, source_target_pairs={{0,48},{48,0},{16,32},{32,16},{1,49},{49,1},{17,33},{33,17},{2,50}... | collective-permute-start | bytes 3145736 | tf_op jit(solution)/shard_map/ppermute | solution.py:238
  33.4 6.5 %collective-permute-start = (bf16[512,128]{1,0:T(8,128)(2,1)S(1)}, bf16[512,128]{1,0:T(8,128)(2,1)S(1)}, u32[]{:S(2)}, u32[]{:S(2)}) collective-permute-start(bf16[512,128]{1,0:T(8,128)(2,1)S(1)} %bitcast.4), channel_id=1, source_target_pairs={{0,16},{16,0},{1,17},{17,1},{2,18},{18,2},{3,19},{19,3},{4,20},{20... | collective-permute-start | bytes 393224 | tf_op jit(solution)/shard_map/ppermute | solution.py:241
  55.5 36.4 %copy-start.2 = (bf16[2048,256]{1,0:T(8,128)(2,1)S(1)}, bf16[2048,256]{1,0:T(8,128)(2,1)}, u32[]{:S(2)}) copy-start(bf16[2048,256]{1,0:T(8,128)(2,1)} %w_ref.1) | copy-start | bytes 3145732

commit v4 on v2

--- a/solution.py
+++ b/solution.py
@@ -12,7 +12,6 @@
 GROUP = 16
 SCALE2 = math.log2(math.e) / math.sqrt(HD)
 XA, XB, ZH, ZL = 2, 2, 4, 4
-OWNERS = XA * XB * ZL
 STAT = 16
 ROWS = HD + STAT
 KEY_BLOCK = 256
@@ -38,20 +37,17 @@
     keys = 2 * near
     blocks = keys // KEY_BLOCK
     x, near_base, far_base, cached_end, span_start = [info_ref[i] for i in range(5)]
-    xb = x & 1
     vt_ref[:HD, :near] = v_ref[...].astype(f32).T.astype(bf16)
     vt_ref[:HD, near:] = kv_ref[:, HD:].astype(f32).T.astype(bf16)
     vt_ref[HD:, :] = jnp.ones((STAT, keys), bf16)
-    chunks = [(q, zl) for q in (0, 1) for zl in range(0, ZL, 2)]
-
-    def query_rows(chunk):
-        q, zl0 = chunk
-        ref = (qa_ref, qb_ref)[q]
+
+    def query_rows(zl):
         parts = []
-        for zl in (zl0, zl0 + 1):
-            for zh in range(ZH):
-                at = (zh * ZL + zl) * 2 * GROUP
-                parts.append(ref[at : at + 2 * GROUP, :])
+        for t in range(2):
+            for ref in (qa_ref, qb_ref):
+                for zh in range(ZH):
+                    at = ((zh * ZL + zl) * 2 + t) * GROUP
+                    parts.append(ref[at : at + GROUP, :])
         return jnp.concatenate(parts, axis=0)
 
     def key_rows(block):
@@ -67,18 +63,16 @@
             visible = (pos < cached_end) | (pos >= span_start) & (pos <= span_start + token)
             hide_ref[half * near : (half + 1) * near, :] = jnp.where(visible, 0.0, HIDDEN).astype(bf16)
 
-    def token_rows(chunk):
-        q, zl0 = chunk
+    def token_rows(zl):
         row = lax.broadcasted_iota(jnp.int32, (2 * HD, HD), 0)
         col = lax.broadcasted_iota(jnp.int32, (2 * HD, HD), 1)
-        owner = x if q == 0 else x ^ 1
-        token = owner * 32 + ((row >> 5) & 3) * 8 + (zl0 + (row >> 7)) * 2 + ((row >> 4) & 1)
-        return jnp.where(token == col, 1.0, 0.0).astype(bf16)
+        t, owner, zh = row >> 7, x ^ ((row >> 6) & 1), (row >> 4) & 3
+        return jnp.where(owner * 32 + zh * 8 + zl * 2 + t == col, 1.0, 0.0).astype(bf16)
 
     def score(i, masked):
-        rows = query_rows(chunks[i])
+        rows = query_rows(i)
         if masked:
-            rows = jnp.concatenate([rows, token_rows(chunks[i])], axis=1)
+            rows = jnp.concatenate([rows, token_rows(i)], axis=1)
         top = None
         for block in range(blocks):
             span = slice(block * KEY_BLOCK, (block + 1) * KEY_BLOCK)
@@ -100,17 +94,15 @@
             part = lax.dot_general(vt_ref[:, span], w, ROW_COL, preferred_element_type=f32)
             total = part if total is None else total + part
         message = pack(total[:HD], top, total[HD : HD + 1])
-        q, zl = chunks[i]
-        to = (xb if q == 0 else 1 - xb) * ZL + zl
-        o_ref[to] = message[:, :HD]
-        o_ref[to + 1] = message[:, HD:]
+        o_ref[i] = message[:, :HD]
+        o_ref[ZL + i] = message[:, HD:]
 
     def run(masked):
         if masked:
             hide()
         top = score(0, masked)
-        for i in range(len(chunks)):
-            following = score(i + 1, masked) if i + 1 < len(chunks) else None
+        for i in range(ZL):
+            following = score(i + 1, masked) if i + 1 < ZL else None
             weigh(i, top)
             top = following
     whole = (near_base + near <= cached_end) & (far_base + near <= cached_end)
@@ -133,24 +125,26 @@
         name="attend",
     )(info, qa, qb, keys, values, far)
 
-def merged(in_ref):
-    senders = in_ref.shape[0]
-    stats = [in_ref[i, HD:, :].astype(f32) for i in range(senders)]
-    tops = [s[0:1] for s in stats]
+def merged(messages):
+    tops = [m[HD : HD + 1] for m in messages]
     top = tops[0]
     for other in tops[1:]:
         top = jnp.maximum(top, other)
     out, total = None, None
-    for i in range(senders):
-        keep = jnp.exp2(tops[i] - top)
-        part = in_ref[i, :HD, :].astype(f32) * keep
-        part_sum = (stats[i][1:2] + stats[i][2:3]) * keep
+    for m, own in zip(messages, tops):
+        keep = jnp.exp2(own - top)
+        part, part_sum = m[:HD] * keep, (m[HD + 1 : HD + 2] + m[HD + 2 : HD + 3]) * keep
         out = part if out is None else out + part
         total = part_sum if total is None else total + part_sum
     return out, top, total
 
+
 def merge_kernel(in_ref, o_ref):
-    message = pack(*merged(in_ref))
+    messages = [in_ref[i].astype(f32) for i in range(XB * ZL)]
+    half = HD // 2
+    for i in range(ZL, XB * ZL):
+        messages[i] = jnp.concatenate([messages[i][:, half:], messages[i][:, :half]], axis=1)
+    message = pack(*merged(messages))
     for i in range(o_ref.shape[0]):
         o_ref[i] = message
 
@@ -165,7 +159,7 @@
     )(came)
 
 def finish_kernel(in_ref, o_ref, turned_ref):
-    out, _, total = merged(in_ref)
+    out, _, total = merged([in_ref[i].astype(f32) for i in range(in_ref.shape[0])])
     turned_ref[...] = (out / total).T
     tokens = o_ref.shape[1]
     heads = [turned_ref[pl.ds(h, tokens, stride=GROUP), :] for h in range(GROUP)]
@@ -184,26 +178,55 @@
         name="finish",
     )(came)
 
-def project_kernel(a_ref, w_ref, o_ref):
-    owners, tokens, depth = a_ref.shape
-    rows = a_ref[...].astype(f32).reshape(owners * tokens, depth).astype(bf16)
-    out = jnp.dot(rows, w_ref[...], preferred_element_type=f32)
-    for x in range(4):
-        for zh in range(ZH):
-            for zl in range(ZL):
-                at = ((x * ZL + zl) * ZH + zh) * 2
-                to = (zh % 2) * 8 + zl * 2
-                o_ref[x * 2 + zh // 2, to : to + 2, :] = out[at : at + 2]
-
-def project(rows, weight):
+def project_kernel(info_ref, a_ref, own_ref, other_ref, o_ref):
+    senders, tokens, depth = a_ref.shape
+    xb = info_ref[0] & 1
+    rows = a_ref[...].astype(f32).reshape(senders * tokens, depth).astype(bf16)
+    for to, w_ref in ((xb, own_ref), (1 - xb, other_ref)):
+        out = jnp.dot(rows, w_ref[...], preferred_element_type=f32)
+        for x in range(XA * XB):
+            for half in range(2):
+                parts = []
+                for zl in range(ZL):
+                    at = (x // XB * ZL + zl) * tokens + x % XB * ZH + half * 2
+                    parts.append(out[at : at + 2])
+                o_ref[(x * 2 + half) * XB + to] = jnp.concatenate(parts, axis=0)
+
+
+def project(info, rows, weight, other):
     return pl.pallas_call(
         project_kernel,
-        out_shape=jax.ShapeDtypeStruct((8, 16, weight.shape[1]), f32),
-        in_specs=in_vmem(2),
+        out_shape=jax.ShapeDtypeStruct((8 * XB, 8, weight.shape[1]), f32),
+        in_specs=[pl.BlockSpec(memory_space=pltpu.SMEM)] + in_vmem(3),
         out_specs=pl.BlockSpec(memory_space=pltpu.VMEM),
         compiler_params=pltpu.CompilerParams(vmem_limit_bytes=8 * MIB),
         name="project",
-    )(rows, weight)
+    )(info, rows, weight, other)
+
+
+def total_kernel(in_ref, o_ref, s_ref):
+    for t in range(2):
+        out = in_ref[t]
+        for sender in range(XB + t, in_ref.shape[0], XB):
+            out = out + in_ref[sender]
+        for zl in range(ZL):
+            for zh in range(2):
+                to = (zh * ZL + zl) * 2 + t
+                s_ref[to : to + 1, :] = out[zl * 2 + zh : zl * 2 + zh + 1]
+    o_ref[...] = s_ref[...].astype(bf16)
+
+
+def total(came):
+    columns = came.shape[2]
+    return pl.pallas_call(
+        total_kernel,
+        out_shape=jax.ShapeDtypeStruct((16, columns), bf16),
+        in_specs=in_vmem(1),
+        out_specs=pl.BlockSpec(memory_space=pltpu.VMEM),
+        scratch_shapes=[pltpu.VMEM((16, columns), f32)],
+        compiler_params=pltpu.CompilerParams(vmem_limit_bytes=2 * MIB),
+        name="total",
+    )(came)
 
 
 def exchange(parts, axes):
@@ -226,13 +249,15 @@
     far = lax.ppermute(cache, ("xa", "xb"), [(0, 3), (3, 0), (1, 2), (2, 1)])
     own = spread(queries.reshape(2 * GROUP, HD), ("zh", "zl"), depth)
     own = own.reshape(depth * 2 * GROUP, HD)
-    other = lax.ppermute(own, "xb", [(0, 1), (1, 0)])
+    swap = [(0, 1), (1, 0)]
+    other = lax.ppermute(own, "xb", swap)
+    other_weight = lax.ppermute(out_weight, "xb", swap)
     parts = attend(info, own, other, cache_keys, cache_values, far)
     came = exchange(parts, ("xb", "zl"))
     came = exchange(merge(came, ZH), ("zh",))
-    attention = exchange(finish(came, OWNERS), ("xa", "xb", "zl"))
-    partial_out = exchange(project(attention, out_weight), ("y", "c"))
-    return jnp.sum(partial_out, axis=0).astype(bf16)
+    attention = exchange(finish(came, XA * ZL), ("xa", "zl"))
+    partial_out = exchange(project(info, attention, out_weight, other_weight), ("y", "c", "xb"))
+    return total(partial_out)
 
 
 def solution(mesh):

time: 108 us -> 109 us (level)
  blocking collectives: 88.6 us -> 55.3 us
  waiting for transfers between devices: 2.4 us -> 21.5 us
  starting transfers between devices: 7.13 us -> 20.6 us
  Pallas kernels: 5.59 us -> 8.33 us
    all_to_all x5 -> x3, blocking collectives: 88.6 us -> 55.3 us  [exchange(): return lax.all_to_all(parts, axes, split_axis=0, concat_axis=0, tiled=True)]
    all_to_all x0 -> x2, waiting for transfers between devices: none -> 16.3 us  [exchange(): return lax.all_to_all(parts, axes, split_axis=0, concat_axis=0, tiled=True)]
    all_to_all x0 -> x2, starting transfers between devices: none -> 11.3 us  [exchange(): return lax.all_to_all(parts, axes, split_axis=0, concat_axis=0, tiled=True)]
    ppermute x1 -> x2, waiting for transfers between devices: 2.39 us -> 5.24 us  [the longest x1 2.85 us: per_device(): other_weight = lax.ppermute(out_weight, 'xb', swap)]
    ppermute x1 -> x2, starting transfers between devices: 1.91 us -> 4.09 us  [the longest x1 2.18 us: per_device(): other_weight = lax.ppermute(out_weight, 'xb', swap)]
    pallas_call x1 -> x2, Pallas kernels: 0.31 us -> 1.65 us  [the longest x1 1.03 us: project(): pl.pallas_call(project_kernel, out_shape=jax.ShapeDtypeStruct((8 * XB, 8,...]
  transfers between devices with their start and end apart: 2 -> 5, of which waited for: 1 -> 4; matrix products, arithmetic and copies ran while one was open for 0% -> 0% of each run, Pallas kernels for 0% -> 1%
where the time goes in v4:
time: 109 us
  blocking collectives  55.3 us (51%)
  waiting for transfers between devices  21.5 us (20%)
  starting transfers between devices  20.6 us (19%)
  Pallas kernels  8.33 us (8%)
  other arithmetic  1.41 us (1%)
  between operations  1.39 us (1%)
    all_to_all x3, blocking collectives, exchange(): return lax.all_to_all(parts, axes, split_axis=0, concat_axis=0, tiled=True)  55.3 us
    all_to_all x2, waiting for transfers between devices, exchange(): return lax.all_to_all(parts, axes, split_axis=0, concat_axis=0, tiled=True)  16.3 us
    all_to_all x2, starting transfers between devices, exchange(): return lax.all_to_all(parts, axes, split_axis=0, concat_axis=0, tiled=True)  11.3 us
    ppermute x1, starting transfers between devices, per_device(): far = lax.ppermute(cache, ('xa', 'xb'), [(0, 3), (3, 0), (1, 2), (2, 1)])  5.22 us
    pallas_call x1, Pallas kernels, attend(): pl.pallas_call(attend_kernel, out_shape=jax.ShapeDtypeStruct((XB * ZL, RO...  5.02 us
    ppermute x1, waiting for transfers between devices, per_device(): other_weight = lax.ppermute(out_weight, 'xb', swap)  2.85 us
    ppermute x1, waiting for transfers between devices, per_device(): other = lax.ppermute(own, 'xb', swap)  2.39 us
  transfers between devices with their start and end apart: 5, of which 4 were waited for; matrix products, arithmetic and copies ran while one was open for 0% of the time, Pallas kernels for 1%

profile of v4, /device:TPU:1, one launch (start us, length us, event | category | flops | bytes accessed | tf_op | source)
XLA Modules:
  0.0 108.7 jit_solution(13763175780390098243)
XLA Ops:
  0.0 0.0 copy-start.1
  0.0 0.0 copy-start
  0.0 0.0 copy-start.3
  0.0 1.4 %pad_maximum_fusion = bf16[2048,256]{1,0:T(8,128)(2,1)S(1)} fusion(bf16[2048,128]{1,0:T(8,128)(2,1)} %v_ref.1, bf16[2048,128]{1,0:T(8,128)(2,1)} %k_ref.1), kind=kLoop, calls=%fused_computation | loop fusion | flops 2097152 | bytes 2097152 | tf_op jit(solution)/shard_map/concatenate | solution.py:247
  1.4 5.2 %collective-permute-start.1 = (bf16[2048,256]{1,0:T(8,128)(2,1)S(1)}, bf16[2048,256]{1,0:T(8,128)(2,1)S(1)}, u32[]{:S(2)}, u32[]{:S(2)}) collective-permute-start(bf16[2048,256]{1,0:T(8,128)(2,1)S(1)} %pad_maximum_fusion), channel_id=1, source_target_pairs={{0,48},{48,0},{16,32},{32,16},{1,49},{49,1},{17,33},{33,17},{2,50}... | collective-permute-start | bytes 3145736 | tf_op jit(solution)/shard_map/ppermute | solution.py:249
  6.6 0.0 copy-done.3
  6.7 26.7 %all_to_all.25 = bf16[16,32,128]{2,1,0:T(8,128)(2,1)S(1)} all-to-all(bf16[16,32,128]{2,1,0:T(8,128)(2,1)S(1)} %broadcast_in_dim.8), channel_id=1, replica_groups=mesh['y'=4,'c'=2,'xa'=2,'xb'=2,'zh'=4,'zl'=4] {'zh','zl'}, dimensions={0} | all-to-all | bytes 262144 | tf_op jit(solution)/shard_map/all_to_all | solution.py:233
  33.4 1.9 %collective-permute-start = (bf16[512,128]{1,0:T(8,128)(2,1)S(1)}, bf16[512,128]{1,0:T(8,128)(2,1)S(1)}, u32[]{:S(2)}, u32[]{:S(2)}) collective-permute-start(bf16[512,128]{1,0:T(8,128)(2,1)S(1)} %bitcast.4), channel_id=1, source_target_pairs={{0,16},{16,0},{1,17},{17,1},{2,18},{18,2},{3,19},{19,3},{4,20},{20... | collective-permute-start | bytes 393224 | tf_op jit(solution)/shard_map/ppermute | solution.py:253
  36.6 0.1 stack.15.info_ref
  36.7 2.4 %collective-permute-done.qb_ref = bf16[512,128]{1,0:T(8,128)(2,1)S(1)} collective-permute-done((bf16[512,128]{1,0:T(8,128)(2,1)S(1)}, bf16[512,128]{1,0:T(8,128)(2,1)S(1)}, u32[]{:S(2)}, u32[]{:S(2)}) %collective-permute-start) | collective-permute-done | bytes 131104 | tf_op jit(solution)/shard_map/ppermute | solution.py:253
  39.1 0.0 collective-permute-done.1.kv_ref
  39.1 0.0 copy-done.1
  39.1 0.0 copy-done
  39.1 5.0 %attend.1 = bf16[8,144,128]{2,1,0:T(8,128)(2,1)S(1)} custom-call(s32[5]{0:T(128)S(1)} %stack.15.info_ref, bf16[512,128]{1,0:T(8,128)(2,1)S(1)} %bitcast.5, bf16[512,128]{1,0:T(8,128)(2,1)S(1)} %collective-permute-done.qb_ref, bf16[2048,128]{1,0:T(8,128)(2,1)S(1)} %copy-done, bf16[2048,128]{1,0:T(8,128)(2,1)S(1)} %copy-done.1, ...), custom_call_target="tpu_custom_call" | custom-call | tf_op jit(solution)/shard_map/attend/pallas_call | solution.py:114
  44.2 0.0 copy-start.2
  44.2 11.6 %all_to_all.26.in_ref = bf16[8,144,128]{2,1,0:T(8,128)(2,1)S(1)} all-to-all(bf16[8,144,128]{2,1,0:T(8,128)(2,1)S(1)} %attend.1), channel_id=1, replica_groups=mesh['y'=4,'c'=2,'xa'=2,'xb'=2,'zh'=4,'zl'=4] {'xb','zl'}, dimensions={0} | all-to-all | bytes 589824 | tf_op jit(solution)/shard_map/all_to_all | solution.py:233
  55.7 0.8 merge.1
  56.5 5.8 %all-to-all-start.2 = ((bf16[4,144,128]{2,1,0:T(8,128)(2,1)}), bf16[4,144,128]{2,1,0:T(8,128)(2,1)S(1)}, u32[]{:S(2)}, u32[]{:S(2)}) async-start(bf16[4,144,128]{2,1,0:T(8,128)(2,1)} %merge.1), calls=%async_computation.2 | async-start | bytes 294912 | tf_op jit(solution)/shard_map/all_to_all | solution.py:233
  62.3 0.0 copy-done.2
  62.3 2.2 %collective-permute-start.2 = (bf16[2048,256]{1,0:T(8,128)(2,1)S(1)}, bf16[2048,256]{1,0:T(8,128)(2,1)S(1)}, u32[]{:S(2)}, u32[]{:S(2)}) collective-permute-start(bf16[2048,256]{1,0:T(8,128)(2,1)S(1)} %copy-done.2), channel_id=1, source_target_pairs={{0,16},{16,0},{1,17},{17,1},{2,18},{18,2},{3,19},{19,3},{4,20},{20... | collective-permute-start | bytes 3145736 | tf_op jit(solution)/shard_map/ppermute | solution.py:254
  64.5 10.1 %all-to-all-done.2.in_ref = bf16[4,144,128]{2,1,0:T(8,128)(2,1)S(1)} async-done(((bf16[4,144,128]{2,1,0:T(8,128)(2,1)}), bf16[4,144,128]{2,1,0:T(8,128)(2,1)S(1)}, u32[]{:S(2)}, u32[]{:S(2)}) %all-to-all-start.2) | async-done | bytes 147488 | tf_op jit(solution)/shard_map/all_to_all | solution.py:233
  74.6 0.9 finish.1
  75.4 5.5 %all-to-all-start.3 = ((bf16[8,8,2048]{2,1,0:T(8,128)(2,1)}), bf16[8,8,2048]{2,1,0:T(8,128)(2,1)S(1)}, u32[]{:S(2)}, u32[]{:S(2)}) async-start(bf16[8,8,2048]{2,1,0:T(8,128)(2,1)} %finish.1), calls=%async_computation.3 | async-start | bytes 524288 | tf_op jit(solution)/shard_map/all_to_all | solution.py:233
  81.0 2.8 %collective-permute-done.2.other_ref = bf16[2048,256]{1,0:T(8,128)(2,1)S(1)} collective-permute-done((bf16[2048,256]{1,0:T(8,128)(2,1)S(1)}, bf16[2048,256]{1,0:T(8,128)(2,1)S(1)}, u32[]{:S(2)}, u32[]{:S(2)}) %collective-permute-start.2) | collective-permute-done | bytes 1048608 | tf_op jit(solution)/shard_map/ppermute | solution.py:254
  83.8 6.2 %all-to-all-done.3.a_ref = bf16[8,8,2048]{2,1,0:T(8,128)(2,1)S(1)} async-done(((bf16[8,8,2048]{2,1,0:T(8,128)(2,1)}), bf16[8,8,2048]{2,1,0:T(8,128)(2,1)S(1)}, u32[]{:S(2)}, u32[]{:S(2)}) %all-to-all-start.3) | async-done | bytes 262176 | tf_op jit(solution)/shard_map/all_to_all | solution.py:233
  90.0 1.0 project.1
  91.0 17.0 %all_to_all.27.in_ref = f32[16,8,256]{2,1,0:T(8,128)S(1)} all-to-all(f32[16,8,256]{2,1,0:T(8,128)S(1)} %project.1), channel_id=1, replica_groups=mesh['y'=4,'c'=2,'xa'=2,'xb'=2,'zh'=4,'zl'=4] {'y','c','xb'}, dimensions={0} | all-to-all | bytes 262144 | tf_op jit(solution)/shard_map/all_to_all | solution.py:233
  108.1 0.6 total.1
  (2 shorter events, 0.0 us)
Async XLA Ops:
  0.0 39.1 %copy-start.1 = (bf16[2048,128]{1,0:T(8,128)(2,1)S(1)}, bf16[2048,128]{1,0:T(8,128)(2,1)}, u32[]{:S(2)}) copy-start(bf16[2048,128]{1,0:T(8,128)(2,1)} %v_ref.1) | copy-start | bytes 1572868
  0.0 39.1 %copy-start = (bf16[2048,128]{1,0:T(8,128)(2,1)S(1)}, bf16[2048,128]{1,0:T(8,128)(2,1)}, u32[]{:S(2)}) copy-start(bf16[2048,128]{1,0:T(8,128)(2,1)} %k_ref.1) | copy-start | bytes 1572868
  0.0 6.6 %copy-start.3 = (bf16[2,2048]{1,0:T(2,128)(2,1)S(1)}, bf16[2,2048]{1,0:T(2,128)(2,1)}, u32[]{:S(2)}) copy-start(bf16[2,2048]{1,0:T(2,128)(2,1)} %param.6) | copy-start | bytes 24580
  1.4 37.7 %collective-permute-start.1 = (bf16[2048,256]{1,0:T(8,128)(2,1)S(1)}, bf16[2048,256]{1,0:T(8,128)(2,1)S(1)}, u32[]{:S(2)}, u32[]{:S(2)}) collective-permute-start(bf16[2048,256]{1,0:T(8,128)(2,1)S(1)} %pad_maximum_fusion), channel_id=1, source_target_pairs={{0,48},{48,0},{16,32},{32,16},{1,49},{49,1},{17,33},{33,17},{2,50}... | collective-permute-start | bytes 3145736 | tf_op jit(solution)/shard_map/ppermute | solution.py:249
  33.4 5.7 %collective-permute-start = (bf16[512,128]{1,0:T(8,128)(2,1)S(1)}, bf16[512,128]{1,0:T(8,128)(2,1)S(1)}, u32[]{:S(2)}, u32[]{:S(2)}) collective-permute-start(bf16[512,128]{1,0:T(8,128)(2,1)S(1)} %bitcast.4), channel_id=1, source_target_pairs={{0,16},{16,0},{1,17},{17,1},{2,18},{18,2},{3,19},{19,3},{4,20},{20... | collective-permute-start | bytes 393224 | tf_op jit(solution)/shard_map/ppermute | solution.py:253
  44.2 18.2 %copy-start.2 = (bf16[2048,256]{1,0:T(8,128)(2,1)S(1)}, bf16[2048,256]{1,0:T(8,128)(2,1)}, u32[]{:S(2)}) copy-start(bf16[2048,256]{1,0:T(8,128)(2,1)} %own_ref.1) | copy-start | bytes 3145732
  56.5 18.0 %all-to-all-start.2 = ((bf16[4,144,128]{2,1,0:T(8,128)(2,1)}), bf16[4,144,128]{2,1,0:T(8,128)(2,1)S(1)}, u32[]{:S(2)}, u32[]{:S(2)}) async-start(bf16[4,144,128]{2,1,0:T(8,128)(2,1)} %merge.1), calls=%async_computation.2 | async-start | bytes 294912 | tf_op jit(solution)/shard_map/all_to_all | solution.py:233
  62.3 21.5 %collective-permute-start.2 = (bf16[2048,256]{1,0:T(8,128)(2,1)S(1)}, bf16[2048,256]{1,0:T(8,128)(2,1)S(1)}, u32[]{:S(2)}, u32[]{:S(2)}) collective-permute-start(bf16[2048,256]{1,0:T(8,128)(2,1)S(1)} %copy-done.2), channel_id=1, source_target_pairs={{0,16},{16,0},{1,17},{17,1},{2,18},{18,2},{3,19},{19,3},{4,20},{20... | collective-permute-start | bytes 3145736 | tf_op jit(solution)/shard_map/ppermute | solution.py:254
  75.4 14.6 %all-to-all-start.3 = ((bf16[8,8,2048]{2,1,0:T(8,128)(2,1)}), bf16[8,8,2048]{2,1,0:T(8,128)(2,1)S(1)}, u32[]{:S(2)}, u32[]{:S(2)}) async-start(bf16[8,8,2048]{2,1,0:T(8,128)(2,1)} %finish.1), calls=%async_computation.3 | async-start | bytes 524288 | tf_op jit(solution)/shard_map/all_to_all | solution.py:233

commit v5 on v4

--- a/solution.py
+++ b/solution.py
@@ -32,14 +32,17 @@
     blank = jnp.zeros((STAT - 3, out.shape[1]), f32)
     return jnp.concatenate([out, top, high, total - high, blank], axis=0).astype(bf16)
 
-def attend_kernel(info_ref, qa_ref, qb_ref, k_ref, v_ref, kv_ref, o_ref, vt_ref, s_ref, hide_ref):
+def attend_kernel(
+    info_ref, qa_ref, qb_ref, k_ref, v_ref, far_ref, o_ref, vt_ref, s_ref, hide_ref, kv_ref, sem
+):
     near = k_ref.shape[0]
     keys = 2 * near
     blocks = keys // KEY_BLOCK
     x, near_base, far_base, cached_end, span_start = [info_ref[i] for i in range(5)]
     vt_ref[:HD, :near] = v_ref[...].astype(f32).T.astype(bf16)
-    vt_ref[:HD, near:] = kv_ref[:, HD:].astype(f32).T.astype(bf16)
     vt_ref[HD:, :] = jnp.ones((STAT, keys), bf16)
+    fetch = pltpu.make_async_copy(far_ref, kv_ref, sem)
+    fetch.start()
 
     def query_rows(zl):
         parts = []
@@ -76,6 +79,9 @@
         top = None
         for block in range(blocks):
             span = slice(block * KEY_BLOCK, (block + 1) * KEY_BLOCK)
+            if i == 0 and block * KEY_BLOCK == near:
+                fetch.wait()
+                vt_ref[:HD, near:] = kv_ref[:, HD:].astype(f32).T.astype(bf16)
             left = key_rows(block)
             if masked:
                 left = jnp.concatenate([left, hide_ref[span, :]], axis=1)
@@ -114,14 +120,18 @@
     return pl.pallas_call(
         attend_kernel,
         out_shape=jax.ShapeDtypeStruct((XB * ZL, ROWS, HD), bf16),
-        in_specs=[pl.BlockSpec(memory_space=pltpu.SMEM)] + in_vmem(5),
+        in_specs=[pl.BlockSpec(memory_space=pltpu.SMEM)]
+        + in_vmem(4)
+        + [pl.BlockSpec(memory_space=pl.ANY)],
         out_specs=pl.BlockSpec(memory_space=pltpu.VMEM),
         scratch_shapes=[
             pltpu.VMEM((ROWS, count), bf16),
             pltpu.VMEM((2, count, 2 * HD), f32),
             pltpu.VMEM((count, HD), bf16),
+            pltpu.VMEM(far.shape, bf16),
+            pltpu.SemaphoreType.DMA,
         ],
-        compiler_params=pltpu.CompilerParams(vmem_limit_bytes=14 * MIB),
+        compiler_params=pltpu.CompilerParams(vmem_limit_bytes=16 * MIB),
         name="attend",
     )(info, qa, qb, keys, values, far)
 
@@ -254,6 +264,7 @@
     other_weight = lax.ppermute(out_weight, "xb", swap)
     parts = attend(info, own, other, cache_keys, cache_values, far)
     came = exchange(parts, ("xb", "zl"))
+    came, other_weight = lax.optimization_barrier((came, other_weight))
     came = exchange(merge(came, ZH), ("zh",))
     attention = exchange(finish(came, XA * ZL), ("xa", "zl"))
     partial_out = exchange(project(info, attention, out_weight, other_weight), ("y", "c", "xb"))

time: 109 us -> 116 us (1.064)
  blocking collectives: 55.3 us -> 75.9 us
  waiting for transfers between devices: 21.5 us -> 12.8 us
  starting transfers between devices: 20.6 us -> 14.5 us
    all_to_all x3 -> x4, blocking collectives: 55.3 us -> 75.9 us  [exchange(): return lax.all_to_all(parts, axes, split_axis=0, concat_axis=0, tiled=True)]
    all_to_all x2 -> x1, waiting for transfers between devices: 16.3 us -> 1.04 us  [exchange(): return lax.all_to_all(parts, axes, split_axis=0, concat_axis=0, tiled=True)]
    ppermute x1, waiting for transfers between devices: 2.85 us -> 11.7 us  [per_device(): other_weight = lax.ppermute(out_weight, 'xb', swap)]
    all_to_all x2 -> x1, starting transfers between devices: 11.3 us -> 3.98 us  [exchange(): return lax.all_to_all(parts, axes, split_axis=0, concat_axis=0, tiled=True)]
    ppermute x1, waiting for transfers between devices: 2.39 us -> 0.01 us  [per_device(): other = lax.ppermute(own, 'xb', swap)]
    pallas_call x1, Pallas kernels: 5.02 us -> 6.56 us  [attend(): pl.pallas_call(attend_kernel, out_shape=jax.ShapeDtypeStruct((XB * ZL, RO...]
    ppermute x1, starting transfers between devices: 2.18 us -> 3.36 us  [per_device(): other_weight = lax.ppermute(out_weight, 'xb', swap)]
  transfers between devices with their start and end apart: 5 -> 4, of which waited for: 4 -> 2; matrix products, arithmetic and copies ran while one was open for 0% -> 0% of each run, Pallas kernels for 1% -> 6%
where the time goes in v5:
time: 116 us
  blocking collectives  75.9 us (65%)
  starting transfers between devices  14.5 us (12%)
  waiting for transfers between devices  12.8 us (11%)
  Pallas kernels  8.5 us (7%)
  other arithmetic  2.49 us (2%)
  between operations  1.42 us (1%)
    all_to_all x4, blocking collectives, exchange(): return lax.all_to_all(parts, axes, split_axis=0, concat_axis=0, tiled=True)  75.9 us
    ppermute x1, waiting for transfers between devices, per_device(): other_weight = lax.ppermute(out_weight, 'xb', swap)  11.7 us
    pallas_call x1, Pallas kernels, attend(): pl.pallas_call(attend_kernel, out_shape=jax.ShapeDtypeStruct((XB * ZL, RO...  6.56 us
    ppermute x1, starting transfers between devices, per_device(): far = lax.ppermute(cache, ('xa', 'xb'), [(0, 3), (3, 0), (1, 2), (2, 1)])  5.21 us
    all_to_all x1, starting transfers between devices, exchange(): return lax.all_to_all(parts, axes, split_axis=0, concat_axis=0, tiled=True)  3.98 us
    ppermute x1, starting transfers between devices, per_device(): other_weight = lax.ppermute(out_weight, 'xb', swap)  3.36 us
    concatenate x1, other arithmetic, per_device(): cache = jnp.concatenate([cache_keys, cache_values], axis=1)  2.49 us
  transfers between devices with their start and end apart: 4, of which 2 were waited for; matrix products, arithmetic and copies ran while one was open for 0% of the time, Pallas kernels for 6%

profile of v5, /device:TPU:1, one launch (start us, length us, event | category | flops | bytes accessed | tf_op | source)
XLA Modules:
  0.0 115.7 jit_solution(4286835241999786724)
XLA Ops:
  0.0 0.0 copy-start.1
  0.0 0.0 copy-start
  0.0 0.0 copy-start.3
  0.0 0.0 copy-start.2
  0.0 2.5 %pad_maximum_fusion = bf16[2048,256]{1,0:T(8,128)(2,1)} fusion(bf16[2048,128]{1,0:T(8,128)(2,1)} %v_ref.1, bf16[2048,128]{1,0:T(8,128)(2,1)} %k_ref.1), kind=kLoop, calls=%fused_computation | loop fusion | flops 2097152 | bytes 2097152 | tf_op jit(solution)/shard_map/concatenate | solution.py:257
  2.5 5.2 %collective-permute-start.1 = (bf16[2048,256]{1,0:T(8,128)(2,1)}, bf16[2048,256]{1,0:T(8,128)(2,1)}, u32[]{:S(2)}, u32[]{:S(2)}) collective-permute-start(bf16[2048,256]{1,0:T(8,128)(2,1)} %pad_maximum_fusion), channel_id=1, source_target_pairs={{0,48},{48,0},{16,32},{32,16},{1,49},{49,1},{17,33},{33,17},{2,50}... | collective-permute-start | bytes 3145736 | tf_op jit(solution)/shard_map/ppermute | solution.py:259
  7.7 0.0 copy-done.3
  7.8 26.7 %all_to_all.25 = bf16[16,32,128]{2,1,0:T(8,128)(2,1)S(1)} all-to-all(bf16[16,32,128]{2,1,0:T(8,128)(2,1)S(1)} %broadcast_in_dim.8), channel_id=1, replica_groups=mesh['y'=4,'c'=2,'xa'=2,'xb'=2,'zh'=4,'zl'=4] {'zh','zl'}, dimensions={0} | all-to-all | bytes 262144 | tf_op jit(solution)/shard_map/all_to_all | solution.py:243
  34.5 1.9 %collective-permute-start = (bf16[512,128]{1,0:T(8,128)(2,1)S(1)}, bf16[512,128]{1,0:T(8,128)(2,1)S(1)}, u32[]{:S(2)}, u32[]{:S(2)}) collective-permute-start(bf16[512,128]{1,0:T(8,128)(2,1)S(1)} %bitcast.4), channel_id=1, source_target_pairs={{0,16},{16,0},{1,17},{17,1},{2,18},{18,2},{3,19},{19,3},{4,20},{20... | collective-permute-start | bytes 393224 | tf_op jit(solution)/shard_map/ppermute | solution.py:263
  36.4 0.0 copy-done.2
  36.4 3.4 %collective-permute-start.2 = (bf16[2048,256]{1,0:T(8,128)(2,1)S(1)}, bf16[2048,256]{1,0:T(8,128)(2,1)S(1)}, u32[]{:S(2)}, u32[]{:S(2)}) collective-permute-start(bf16[2048,256]{1,0:T(8,128)(2,1)S(1)} %copy-done.2), channel_id=1, source_target_pairs={{0,16},{16,0},{1,17},{17,1},{2,18},{18,2},{3,19},{19,3},{4,20},{20... | collective-permute-start | bytes 3145736 | tf_op jit(solution)/shard_map/ppermute | solution.py:264
  41.1 0.1 stack.15.info_ref
  41.2 0.0 collective-permute-done.qb_ref
  41.2 0.0 collective-permute-done.1.far_ref
  41.2 0.0 copy-done.1
  41.2 0.0 copy-done
  41.2 6.6 %attend.1 = bf16[8,144,128]{2,1,0:T(8,128)(2,1)} custom-call(s32[5]{0:T(128)S(1)} %stack.15.info_ref, bf16[512,128]{1,0:T(8,128)(2,1)S(1)} %bitcast.5, bf16[512,128]{1,0:T(8,128)(2,1)S(1)} %collective-permute-done.qb_ref, bf16[2048,128]{1,0:T(8,128)(2,1)S(1)} %copy-done, bf16[2048,128]{1,0:T(8,128)(2,1)S(1)} %copy-done.1, ...), custom_call_target="tpu_custom_call" | custom-call | tf_op jit(solution)/shard_map/attend/pallas_call | solution.py:120
  47.8 4.0 %all-to-all-start.1 = ((bf16[8,144,128]{2,1,0:T(8,128)(2,1)}), bf16[8,144,128]{2,1,0:T(8,128)(2,1)S(1)}, u32[]{:S(2)}, u32[]{:S(2)}) async-start(bf16[8,144,128]{2,1,0:T(8,128)(2,1)} %attend.1), calls=%async_computation.1 | async-start | bytes 589824 | tf_op jit(solution)/shard_map/all_to_all | solution.py:243
  51.7 11.7 %collective-permute-done.2.other_ref = bf16[2048,256]{1,0:T(8,128)(2,1)S(1)} collective-permute-done((bf16[2048,256]{1,0:T(8,128)(2,1)S(1)}, bf16[2048,256]{1,0:T(8,128)(2,1)S(1)}, u32[]{:S(2)}, u32[]{:S(2)}) %collective-permute-start.2) | collective-permute-done | bytes 1048608 | tf_op jit(solution)/shard_map/ppermute | solution.py:264
  63.5 1.0 all-to-all-done.1.in_ref
  64.5 0.1 merge.1
  64.6 19.8 %all_to_all.26.in_ref = bf16[4,144,128]{2,1,0:T(8,128)(2,1)S(1)} all-to-all(bf16[4,144,128]{2,1,0:T(8,128)(2,1)S(1)} %merge.1), channel_id=1, replica_groups=mesh['y'=4,'c'=2,'xa'=2,'xb'=2,'zh'=4,'zl'=4] {'zh'}, dimensions={0} | all-to-all | bytes 294912 | tf_op jit(solution)/shard_map/all_to_all | solution.py:243
  84.4 0.1 finish.1
  84.6 14.4 %all_to_all.27.a_ref = bf16[8,8,2048]{2,1,0:T(8,128)(2,1)S(1)} all-to-all(bf16[8,8,2048]{2,1,0:T(8,128)(2,1)S(1)} %finish.1), channel_id=1, replica_groups=mesh['y'=4,'c'=2,'xa'=2,'xb'=2,'zh'=4,'zl'=4] {'xa','zl'}, dimensions={0} | all-to-all | bytes 524288 | tf_op jit(solution)/shard_map/all_to_all | solution.py:243
  99.0 1.0 project.1
  100.0 15.1 %all_to_all.28.in_ref = f32[16,8,256]{2,1,0:T(8,128)S(1)} all-to-all(f32[16,8,256]{2,1,0:T(8,128)S(1)} %project.1), channel_id=1, replica_groups=mesh['y'=4,'c'=2,'xa'=2,'xb'=2,'zh'=4,'zl'=4] {'y','c','xb'}, dimensions={0} | all-to-all | bytes 262144 | tf_op jit(solution)/shard_map/all_to_all | solution.py:243
  115.1 0.6 total.1
  (2 shorter events, 0.0 us)
Async XLA Ops:
  0.0 41.2 %copy-start.1 = (bf16[2048,128]{1,0:T(8,128)(2,1)S(1)}, bf16[2048,128]{1,0:T(8,128)(2,1)}, u32[]{:S(2)}) copy-start(bf16[2048,128]{1,0:T(8,128)(2,1)} %v_ref.1) | copy-start | bytes 1572868
  0.0 41.2 %copy-start = (bf16[2048,128]{1,0:T(8,128)(2,1)S(1)}, bf16[2048,128]{1,0:T(8,128)(2,1)}, u32[]{:S(2)}) copy-start(bf16[2048,128]{1,0:T(8,128)(2,1)} %k_ref.1) | copy-start | bytes 1572868
  0.0 7.7 %copy-start.3 = (bf16[2,2048]{1,0:T(2,128)(2,1)S(1)}, bf16[2,2048]{1,0:T(2,128)(2,1)}, u32[]{:S(2)}) copy-start(bf16[2,2048]{1,0:T(2,128)(2,1)} %param.6) | copy-start | bytes 24580
  0.0 36.4 %copy-start.2 = (bf16[2048,256]{1,0:T(8,128)(2,1)S(1)}, bf16[2048,256]{1,0:T(8,128)(2,1)}, u32[]{:S(2)}) copy-start(bf16[2048,256]{1,0:T(8,128)(2,1)} %own_ref.1) | copy-start | bytes 3145732
  2.5 38.7 %collective-permute-start.1 = (bf16[2048,256]{1,0:T(8,128)(2,1)}, bf16[2048,256]{1,0:T(8,128)(2,1)}, u32[]{:S(2)}, u32[]{:S(2)}) collective-permute-start(bf16[2048,256]{1,0:T(8,128)(2,1)} %pad_maximum_fusion), channel_id=1, source_target_pairs={{0,48},{48,0},{16,32},{32,16},{1,49},{49,1},{17,33},{33,17},{2,50}... | collective-permute-start | bytes 3145736 | tf_op jit(solution)/shard_map/ppermute | solution.py:259
  34.5 6.7 %collective-permute-start = (bf16[512,128]{1,0:T(8,128)(2,1)S(1)}, bf16[512,128]{1,0:T(8,128)(2,1)S(1)}, u32[]{:S(2)}, u32[]{:S(2)}) collective-permute-start(bf16[512,128]{1,0:T(8,128)(2,1)S(1)} %bitcast.4), channel_id=1, source_target_pairs={{0,16},{16,0},{1,17},{17,1},{2,18},{18,2},{3,19},{19,3},{4,20},{20... | collective-permute-start | bytes 393224 | tf_op jit(solution)/shard_map/ppermute | solution.py:263
  36.4 27.1 %collective-permute-start.2 = (bf16[2048,256]{1,0:T(8,128)(2,1)S(1)}, bf16[2048,256]{1,0:T(8,128)(2,1)S(1)}, u32[]{:S(2)}, u32[]{:S(2)}) collective-permute-start(bf16[2048,256]{1,0:T(8,128)(2,1)S(1)} %copy-done.2), channel_id=1, source_target_pairs={{0,16},{16,0},{1,17},{17,1},{2,18},{18,2},{3,19},{19,3},{4,20},{20... | collective-permute-start | bytes 3145736 | tf_op jit(solution)/shard_map/ppermute | solution.py:264
  47.8 16.7 %all-to-all-start.1 = ((bf16[8,144,128]{2,1,0:T(8,128)(2,1)}), bf16[8,144,128]{2,1,0:T(8,128)(2,1)S(1)}, u32[]{:S(2)}, u32[]{:S(2)}) async-start(bf16[8,144,128]{2,1,0:T(8,128)(2,1)} %attend.1), calls=%async_computation.1 | async-start | bytes 589824 | tf_op jit(solution)/shard_map/all_to_all | solution.py:243

commit v6 on v2

--- a/solution.py
+++ b/solution.py
@@ -11,14 +11,20 @@
 HD = 128
 GROUP = 16
 SCALE2 = math.log2(math.e) / math.sqrt(HD)
-XA, XB, ZH, ZL = 2, 2, 4, 4
-OWNERS = XA * XB * ZL
+X, ZH, ZL = 4, 4, 4
+OWNERS = X * ZL
 STAT = 16
 ROWS = HD + STAT
 KEY_BLOCK = 256
 HIDDEN = -1e30
 LOWEST = -1e5
 MIB = 2**20
+SHARE = [(x, x ^ 1) for x in range(X)] + [(X + x, X + 3 - x) for x in range(X)]
+SWAP = [(x, 3 - x) for x in range(X)] + [(X + x, X + (x ^ 1)) for x in range(X)]
+OWNER_GROUPS = [
+    [(c * X + x) * ZL + zl for x in xs for zl in range(ZL)]
+    for c, xs in ((0, (0, 1)), (0, (2, 3)), (1, (0, 3)), (1, (1, 2)))
+]
 
 bf16 = jnp.bfloat16
 f32 = jnp.float32
@@ -33,14 +39,15 @@
     blank = jnp.zeros((STAT - 3, out.shape[1]), f32)
     return jnp.concatenate([out, top, high, total - high, blank], axis=0).astype(bf16)
 
-def attend_kernel(info_ref, qa_ref, qb_ref, k_ref, v_ref, kv_ref, o_ref, vt_ref, s_ref, hide_ref):
+def attend_kernel(
+    info_ref, qa_ref, qb_ref, k_ref, v_ref, kf_ref, vf_ref, o_ref, vt_ref, s_ref, hide_ref
+):
     near = k_ref.shape[0]
     keys = 2 * near
     blocks = keys // KEY_BLOCK
-    x, near_base, far_base, cached_end, span_start = [info_ref[i] for i in range(5)]
-    xb = x & 1
+    x, pair, rank, near_base, far_base, cached_end, span_start = [info_ref[i] for i in range(7)]
     vt_ref[:HD, :near] = v_ref[...].astype(f32).T.astype(bf16)
-    vt_ref[:HD, near:] = kv_ref[:, HD:].astype(f32).T.astype(bf16)
+    vt_ref[:HD, near:] = vf_ref[...].astype(f32).T.astype(bf16)
     vt_ref[HD:, :] = jnp.ones((STAT, keys), bf16)
     chunks = [(q, zl) for q in (0, 1) for zl in range(0, ZL, 2)]
 
@@ -58,7 +65,7 @@
         at = block * KEY_BLOCK
         if at < near:
             return k_ref[at : at + KEY_BLOCK, :]
-        return kv_ref[at - near : at - near + KEY_BLOCK, :HD]
+        return kf_ref[at - near : at - near + KEY_BLOCK, :]
 
     def hide():
         for half, base in ((0, near_base), (1, far_base)):
@@ -71,7 +78,7 @@
         q, zl0 = chunk
         row = lax.broadcasted_iota(jnp.int32, (2 * HD, HD), 0)
         col = lax.broadcasted_iota(jnp.int32, (2 * HD, HD), 1)
-        owner = x if q == 0 else x ^ 1
+        owner = x if q == 0 else pair
         token = owner * 32 + ((row >> 5) & 3) * 8 + (zl0 + (row >> 7)) * 2 + ((row >> 4) & 1)
         return jnp.where(token == col, 1.0, 0.0).astype(bf16)
 
@@ -101,7 +108,7 @@
             total = part if total is None else total + part
         message = pack(total[:HD], top, total[HD : HD + 1])
         q, zl = chunks[i]
-        to = (xb if q == 0 else 1 - xb) * ZL + zl
+        to = (rank if q == 0 else 1 - rank) * ZL + zl
         o_ref[to] = message[:, :HD]
         o_ref[to + 1] = message[:, HD:]
 
@@ -117,12 +124,12 @@
     pl.when(whole)(lambda: run(False))
     pl.when(jnp.logical_not(whole))(lambda: run(True))
 
-def attend(info, qa, qb, keys, values, far):
+def attend(info, qa, qb, keys, values, far_keys, far_values):
     count = 2 * keys.shape[0]
     return pl.pallas_call(
         attend_kernel,
-        out_shape=jax.ShapeDtypeStruct((XB * ZL, ROWS, HD), bf16),
-        in_specs=[pl.BlockSpec(memory_space=pltpu.SMEM)] + in_vmem(5),
+        out_shape=jax.ShapeDtypeStruct((2 * ZL, ROWS, HD), bf16),
+        in_specs=[pl.BlockSpec(memory_space=pltpu.SMEM)] + in_vmem(6),
         out_specs=pl.BlockSpec(memory_space=pltpu.VMEM),
         scratch_shapes=[
             pltpu.VMEM((ROWS, count), bf16),
@@ -131,7 +138,7 @@
         ],
         compiler_params=pltpu.CompilerParams(vmem_limit_bytes=14 * MIB),
         name="attend",
-    )(info, qa, qb, keys, values, far)
+    )(info, qa, qb, keys, values, far_keys, far_values)
 
 def merged(in_ref):
     senders = in_ref.shape[0]
@@ -206,8 +213,10 @@
     )(rows, weight)
 
 
-def exchange(parts, axes):
-    return lax.all_to_all(parts, axes, split_axis=0, concat_axis=0, tiled=True)
+def exchange(parts, axes, groups=None):
+    return lax.all_to_all(
+        parts, axes, split_axis=0, concat_axis=0, axis_index_groups=groups, tiled=True
+    )
 
 
 def spread(part, axes, count):
@@ -216,29 +225,30 @@
 
 def per_device(queries, cache_keys, cache_values, out_weight, cached_length, start):
     count = cache_keys.shape[0]
-    x = lax.axis_index(("xa", "xb"))
+    x, c = lax.axis_index("x"), lax.axis_index("c")
     z = lax.axis_index(("zh", "zl"))
     depth = ZH * ZL
-    near_base, far_base = (x * depth + z) * count, ((3 - x) * depth + z) * count
-    info = jnp.stack([x, near_base, far_base, cached_length[0], start[0]]).astype(jnp.int32)
-    cache = jnp.concatenate([cache_keys, cache_values], axis=1)
-    cache, queries = lax.optimization_barrier((cache, queries))
-    far = lax.ppermute(cache, ("xa", "xb"), [(0, 3), (3, 0), (1, 2), (2, 1)])
+    pair, far_x = jnp.where(c == 0, x ^ 1, 3 - x), jnp.where(c == 0, 3 - x, x ^ 1)
+    rank = jnp.where(c == 0, x & 1, x >> 1)
+    near_base, far_base = (x * depth + z) * count, (far_x * depth + z) * count
+    info = jnp.stack([x, pair, rank, near_base, far_base, cached_length[0], start[0]])
+    info = info.astype(jnp.int32)
+    far_keys = lax.ppermute(cache_keys, ("c", "x"), SWAP)
+    far_values = lax.ppermute(cache_values, ("c", "x"), SWAP)
     own = spread(queries.reshape(2 * GROUP, HD), ("zh", "zl"), depth)
     own = own.reshape(depth * 2 * GROUP, HD)
-    other = lax.ppermute(own, "xb", [(0, 1), (1, 0)])
-    parts = attend(info, own, other, cache_keys, cache_values, far)
-    came = exchange(parts, ("xb", "zl"))
+    other = lax.ppermute(own, ("c", "x"), SHARE)
+    parts = attend(info, own, other, cache_keys, cache_values, far_keys, far_values)
+    came = exchange(parts, ("c", "x", "zl"), OWNER_GROUPS)
     came = exchange(merge(came, ZH), ("zh",))
-    attention = exchange(finish(came, OWNERS), ("xa", "xb", "zl"))
+    attention = exchange(finish(came, OWNERS), ("x", "zl"))
     partial_out = exchange(project(attention, out_weight), ("y", "c"))
     return jnp.sum(partial_out, axis=0).astype(bf16)
 
 
 def solution(mesh):
-    shape = (4, 2, XA, XB, ZH, ZL)
-    fine = Mesh(mesh.devices.reshape(shape), ("y", "c", "xa", "xb", "zh", "zl"))
-    ctx, kv = ("xa", "xb", "zh", "zl"), ("y", "c")
+    fine = Mesh(mesh.devices.reshape(4, 2, X, ZH, ZL), ("y", "c", "x", "zh", "zl"))
+    ctx, kv = ("x", "zh", "zl"), ("y", "c")
     return jax.shard_map(
         per_device,
         mesh=fine,

time: 108 us -> 111 us (1.028)
  blocking collectives: 88.6 us -> 65.5 us
  starting transfers between devices: 7.13 us -> 25.4 us
  waiting for transfers between devices: 2.4 us -> 8.7 us
  local copies, waits for them, and re-layouts: 0.13 us -> 3.55 us
  other arithmetic: 2.02 us -> 0.61 us
    all_to_all x5 -> x4, blocking collectives: 88.6 us -> 65.5 us  [exchange(): lax.all_to_all(parts, axes, split_axis=0, concat_axis=0, axis_index_group...]
    all_to_all x0 -> x1, starting transfers between devices: none -> 15.7 us  [exchange(): lax.all_to_all(parts, axes, split_axis=0, concat_axis=0, axis_index_group...]
    all_to_all x0 -> x1, waiting for transfers between devices: none -> 6.7 us  [exchange(): lax.all_to_all(parts, axes, split_axis=0, concat_axis=0, axis_index_group...]
    ppermute x2 -> x3, starting transfers between devices: 7.13 us -> 9.66 us  [the longest x1 4.38 us: per_device(): other = lax.ppermute(own, ('c', 'x'), SHARE)]
    unnamed x8 -> x6, local copies, waits for them, and re-layouts: 0.02 us -> 2.09 us
    concatenate x1 -> x0, other arithmetic: 1.41 us -> none  [per_device(): cache = jnp.concatenate([cache_keys, cache_values], axis=1)]
    broadcast_in_dim x2, local copies, waits for them, and re-layouts: 0.03 us -> 1.37 us  [spread(): return exchange(jnp.broadcast_to(part[None], (count,) + part.shape), axes)]
    ppermute x2 -> x3, waiting for transfers between devices: 2.4 us -> 2 us  [the longest x1 2 us: per_device(): other = lax.ppermute(own, ('c', 'x'), SHARE)]
  transfers between devices with their start and end apart: 2 -> 4, of which waited for: 1 -> 2; matrix products, arithmetic and copies ran while one was open for 0% -> 0% of each run, Pallas kernels for 0% -> 0%
where the time goes in v6:
time: 111 us
  blocking collectives  65.5 us (59%)
  starting transfers between devices  25.4 us (23%)
  waiting for transfers between devices  8.7 us (8%)
  Pallas kernels  5.61 us (5%)
  local copies, waits for them, and re-layouts  3.55 us (3%)
  between operations  1.39 us (1%)
    all_to_all x4, blocking collectives, exchange(): lax.all_to_all(parts, axes, split_axis=0, concat_axis=0, axis_index_group...  65.5 us
    all_to_all x1, starting transfers between devices, exchange(): lax.all_to_all(parts, axes, split_axis=0, concat_axis=0, axis_index_group...  15.7 us
    all_to_all x1, waiting for transfers between devices, exchange(): lax.all_to_all(parts, axes, split_axis=0, concat_axis=0, axis_index_group...  6.7 us
    pallas_call x1, Pallas kernels, attend(): pl.pallas_call(attend_kernel, out_shape=jax.ShapeDtypeStruct((2 * ZL, ROW...  5.04 us
    ppermute x1, starting transfers between devices, per_device(): other = lax.ppermute(own, ('c', 'x'), SHARE)  4.38 us
    ppermute x1, starting transfers between devices, per_device(): far_keys = lax.ppermute(cache_keys, ('c', 'x'), SWAP)  3.12 us
  transfers between devices with their start and end apart: 4, of which 2 were waited for; matrix products, arithmetic and copies ran while one was open for 0% of the time, Pallas kernels for 0%

profile of v6, /device:TPU:1, one launch (start us, length us, event | category | flops | bytes accessed | tf_op | source)
XLA Modules:
  0.0 110.7 jit_solution(10676772486304104847)
XLA Ops:
  0.0 0.7 broadcast_in_dim.7
  0.7 0.7 broadcast_in_dim.8
  1.4 15.7 %all-to-all-start = ((bf16[16,32,128]{2,1,0:T(8,128)(2,1)}), bf16[16,32,128]{2,1,0:T(8,128)(2,1)S(1)}, u32[]{:S(2)}, u32[]{:S(2)}) async-start(bf16[16,32,128]{2,1,0:T(8,128)(2,1)} %broadcast_in_dim.8), calls=%async_computation | async-start | bytes 262144 | tf_op jit(solution)/shard_map/all_to_all | solution.py:217
  17.1 3.1 %collective-permute-start.1 = (bf16[2048,128]{1,0:T(8,128)(2,1)}, bf16[2048,128]{1,0:T(8,128)(2,1)S(1)}, u32[]{:S(2)}, u32[]{:S(2)}) collective-permute-start(bf16[2048,128]{1,0:T(8,128)(2,1)} %k_ref.1), channel_id=1, source_target_pairs={{0,48},{16,32},{32,16},{48,0},{64,80},{80,64},{96,112},{112,96},{1... | collective-permute-start | bytes 1572872 | tf_op jit(solution)/shard_map/ppermute | solution.py:236
  20.3 2.2 %collective-permute-start.2 = (bf16[2048,128]{1,0:T(8,128)(2,1)}, bf16[2048,128]{1,0:T(8,128)(2,1)S(1)}, u32[]{:S(2)}, u32[]{:S(2)}) collective-permute-start(bf16[2048,128]{1,0:T(8,128)(2,1)} %v_ref.1), channel_id=1, source_target_pairs={{0,48},{16,32},{32,16},{48,0},{64,80},{80,64},{96,112},{112,96},{1... | collective-permute-start | bytes 1572872 | tf_op jit(solution)/shard_map/ppermute | solution.py:237
  22.4 6.7 %all-to-all-done = bf16[16,32,128]{2,1,0:T(8,128)(2,1)S(1)} async-done(((bf16[16,32,128]{2,1,0:T(8,128)(2,1)}), bf16[16,32,128]{2,1,0:T(8,128)(2,1)S(1)}, u32[]{:S(2)}, u32[]{:S(2)}) %all-to-all-start) | async-done | bytes 131104 | tf_op jit(solution)/shard_map/all_to_all | solution.py:217
  29.1 4.4 %collective-permute-start = (bf16[512,128]{1,0:T(8,128)(2,1)S(1)}, bf16[512,128]{1,0:T(8,128)(2,1)S(1)}, u32[]{:S(2)}, u32[]{:S(2)}) collective-permute-start(bf16[512,128]{1,0:T(8,128)(2,1)S(1)} %bitcast.6), channel_id=1, source_target_pairs={{0,16},{16,0},{32,48},{48,32},{64,112},{80,96},{96,80},{112,64},{1... | collective-permute-start | bytes 393224 | tf_op jit(solution)/shard_map/ppermute | solution.py:240
  34.8 0.1 stack.23.info_ref
  34.9 0.0 collective-permute-done.1.kf_ref
  34.9 0.0 collective-permute-done.2.vf_ref
  34.9 2.0 %collective-permute-done.qb_ref = bf16[512,128]{1,0:T(8,128)(2,1)S(1)} collective-permute-done((bf16[512,128]{1,0:T(8,128)(2,1)S(1)}, bf16[512,128]{1,0:T(8,128)(2,1)S(1)}, u32[]{:S(2)}, u32[]{:S(2)}) %collective-permute-start) | collective-permute-done | bytes 131104 | tf_op jit(solution)/shard_map/ppermute | solution.py:240
  36.9 0.0 copy-start.1
  36.9 1.0 copy-done.1
  38.0 0.0 copy-start.2
  38.0 1.0 copy-done.2
  39.0 5.0 %attend.1 = bf16[8,144,128]{2,1,0:T(8,128)(2,1)S(1)} custom-call(s32[7]{0:T(128)S(1)} %stack.23.info_ref, bf16[512,128]{1,0:T(8,128)(2,1)S(1)} %bitcast.7, bf16[512,128]{1,0:T(8,128)(2,1)S(1)} %collective-permute-done.qb_ref, bf16[2048,128]{1,0:T(8,128)(2,1)S(1)} %copy-done.1, bf16[2048,128]{1,0:T(8,128)(2,1)S(1)} %copy-done.2, ...), custom_call_target="tpu_custom_call" | custom-call | tf_op jit(solution)/shard_map/attend/pallas_call | solution.py:129
  44.0 18.3 %all_to_all.25.in_ref = bf16[8,144,128]{2,1,0:T(8,128)(2,1)S(1)} all-to-all(bf16[8,144,128]{2,1,0:T(8,128)(2,1)S(1)} %attend.1), channel_id=1, replica_groups={{0,1,2,3,16,17,18,19},{32,33,34,35,48,49,50,51},{64,65,66,67,112,113,11..., dimensions={0} | all-to-all | bytes 589824 | tf_op jit(solution)/shard_map/all_to_all | solution.py:217
  62.3 0.1 merge.1
  62.4 0.0 copy-start
  62.4 17.3 %all_to_all.26.in_ref = bf16[4,144,128]{2,1,0:T(8,128)(2,1)S(1)} all-to-all(bf16[4,144,128]{2,1,0:T(8,128)(2,1)S(1)} %merge.1), channel_id=1, replica_groups=mesh['y'=4,'c'=2,'x'=4,'zh'=4,'zl'=4] {'zh'}, dimensions={0} | all-to-all | bytes 294912 | tf_op jit(solution)/shard_map/all_to_all | solution.py:217
  79.7 0.2 finish.1
  79.9 14.4 %all_to_all.27.a_ref = bf16[16,8,2048]{2,1,0:T(8,128)(2,1)S(1)} all-to-all(bf16[16,8,2048]{2,1,0:T(8,128)(2,1)S(1)} %finish.1), channel_id=1, replica_groups=mesh['y'=4,'c'=2,'x'=4,'zh'=4,'zl'=4] {'x','zl'}, dimensions={0} | all-to-all | bytes 1048576 | tf_op jit(solution)/shard_map/all_to_all | solution.py:217
  94.3 0.0 copy-done
  94.3 0.3 project.1
  94.6 15.5 %all_to_all.28 = f32[8,16,256]{2,1,0:T(8,128)S(1)} all-to-all(f32[8,16,256]{2,1,0:T(8,128)S(1)} %project.1), channel_id=1, replica_groups=mesh['y'=4,'c'=2,'x'=4,'zh'=4,'zl'=4] {'y','c'}, dimensions={0} | all-to-all | bytes 262144 | tf_op jit(solution)/shard_map/all_to_all | solution.py:217
  110.1 0.6 reduce_sum.9
Async XLA Ops:
  1.4 27.8 %all-to-all-start = ((bf16[16,32,128]{2,1,0:T(8,128)(2,1)}), bf16[16,32,128]{2,1,0:T(8,128)(2,1)S(1)}, u32[]{:S(2)}, u32[]{:S(2)}) async-start(bf16[16,32,128]{2,1,0:T(8,128)(2,1)} %broadcast_in_dim.8), calls=%async_computation | async-start | bytes 262144 | tf_op jit(solution)/shard_map/all_to_all | solution.py:217
  17.1 17.8 %collective-permute-start.1 = (bf16[2048,128]{1,0:T(8,128)(2,1)}, bf16[2048,128]{1,0:T(8,128)(2,1)S(1)}, u32[]{:S(2)}, u32[]{:S(2)}) collective-permute-start(bf16[2048,128]{1,0:T(8,128)(2,1)} %k_ref.1), channel_id=1, source_target_pairs={{0,48},{16,32},{32,16},{48,0},{64,80},{80,64},{96,112},{112,96},{1... | collective-permute-start | bytes 1572872 | tf_op jit(solution)/shard_map/ppermute | solution.py:236
  20.3 14.7 %collective-permute-start.2 = (bf16[2048,128]{1,0:T(8,128)(2,1)}, bf16[2048,128]{1,0:T(8,128)(2,1)S(1)}, u32[]{:S(2)}, u32[]{:S(2)}) collective-permute-start(bf16[2048,128]{1,0:T(8,128)(2,1)} %v_ref.1), channel_id=1, source_target_pairs={{0,48},{16,32},{32,16},{48,0},{64,80},{80,64},{96,112},{112,96},{1... | collective-permute-start | bytes 1572872 | tf_op jit(solution)/shard_map/ppermute | solution.py:237
  29.1 7.8 %collective-permute-start = (bf16[512,128]{1,0:T(8,128)(2,1)S(1)}, bf16[512,128]{1,0:T(8,128)(2,1)S(1)}, u32[]{:S(2)}, u32[]{:S(2)}) collective-permute-start(bf16[512,128]{1,0:T(8,128)(2,1)S(1)} %bitcast.6), channel_id=1, source_target_pairs={{0,16},{16,0},{32,48},{48,32},{64,112},{80,96},{96,80},{112,64},{1... | collective-permute-start | bytes 393224 | tf_op jit(solution)/shard_map/ppermute | solution.py:240
  36.9 1.0 copy-start.1
  38.0 1.0 copy-start.2
  62.4 31.8 %copy-start = (bf16[2048,256]{1,0:T(8,128)(2,1)S(1)}, bf16[2048,256]{1,0:T(8,128)(2,1)}, u32[]{:S(2)}) copy-start(bf16[2048,256]{1,0:T(8,128)(2,1)} %w_ref.1) | copy-start | bytes 3145732

commit v7 on v3

--- a/solution.py
+++ b/solution.py
@@ -12,14 +12,20 @@
 HD = 128
 GROUP = 16
 SCALE2 = math.log2(math.e) / math.sqrt(HD)
-XA, XB, ZH, ZL = 2, 2, 4, 4
-OWNERS = XA * XB * ZL
+X, ZH, ZL = 4, 4, 4
+OWNERS = X * ZL
 STAT = 16
 ROWS = HD + STAT
 KEY_BLOCK = 256
 HIDDEN = -1e30
 LOWEST = -1e5
 MIB = 2**20
+SHARE = [(x, x ^ 1) for x in range(X)] + [(X + x, X + 3 - x) for x in range(X)]
+SWAP = [(x, 3 - x) for x in range(X)] + [(X + x, X + (x ^ 1)) for x in range(X)]
+OWNER_GROUPS = [
+    [(c * X + x) * ZL + zl for x in xs for zl in range(ZL)]
+    for c, xs in ((0, (0, 1)), (0, (2, 3)), (1, (0, 3)), (1, (1, 2)))
+]
 
 bf16 = jnp.bfloat16
 f32 = jnp.float32
@@ -40,9 +46,10 @@
     else:
         vt_ref, hide_ref, _, o_ref, s_ref = refs
     near = k_ref.shape[0]
-    blocks = 2 * near // KEY_BLOCK
-    x, near_base, far_base, cached_end, span_start = [info_ref[i] for i in range(5)]
-    owner = x if own else x ^ 1
+    blocks = near // KEY_BLOCK
+    x, pair, rank, near_base, far_base, cached_end, span_start = [info_ref[i] for i in range(7)]
+    owner, to_rank = (x, rank) if own else (pair, 1 - rank)
+    chunks = [(zl0, half) for zl0 in range(0, ZL, 2) for half in range(2)]
 
     def query_rows(zl0):
         parts = []
@@ -52,11 +59,8 @@
                 parts.append(q_ref[at : at + 2 * GROUP, :])
         return jnp.concatenate(parts, axis=0)
 
-    def key_rows(block):
-        at = block * KEY_BLOCK
-        if at < near:
-            return k_ref[at : at + KEY_BLOCK, :]
-        return far_ref[at - near : at - near + KEY_BLOCK, :HD]
+    def key_rows(half, span):
+        return k_ref[span, :] if half == 0 else far_ref[span, :HD]
 
     def hide():
         for half, base in ((0, near_base), (1, far_base)):
@@ -72,46 +76,60 @@
         zh, zl, t = (row >> 5) & 3, zl0 + (row >> 7), (row >> 4) & 1
         return jnp.where(owner * 32 + zh * 8 + zl * 2 + t == col, 1.0, 0.0).astype(bf16)
 
-    def score(zl0, slot, masked):
+    def score(i, masked):
+        zl0, half = chunks[i]
         rows = query_rows(zl0)
         if masked:
             rows = jnp.concatenate([rows, token_rows(zl0)], axis=1)
         top = None
         for block in range(blocks):
-            span = slice(block * KEY_BLOCK, (block + 1) * KEY_BLOCK)
-            left = key_rows(block)
+            at = block * KEY_BLOCK
+            left = key_rows(half, slice(at, at + KEY_BLOCK))
             if masked:
-                left = jnp.concatenate([left, hide_ref[span, :]], axis=1)
+                at += half * near
+                left = jnp.concatenate([left, hide_ref[at : at + KEY_BLOCK, :]], axis=1)
             s = lax.dot_general(left, rows, ROW_ROW, preferred_element_type=f32)
-            s_ref[slot, span, :] = s
+            s_ref[i % 2, block * KEY_BLOCK : (block + 1) * KEY_BLOCK, :] = s
             here = jnp.max(s.reshape(KEY_BLOCK // 8, 8, s.shape[1]), axis=0)
             top = here if top is None else jnp.maximum(top, here)
         top = jnp.max(top, axis=0, keepdims=True) * SCALE2
         return jnp.maximum(top, LOWEST).astype(bf16).astype(f32)
 
-    def weigh(zl0, slot, top):
+    def weigh(i, top):
+        half = chunks[i][1]
         total = None
         for block in range(blocks):
-            span = slice(block * KEY_BLOCK, (block + 1) * KEY_BLOCK)
-            w = jnp.exp2(s_ref[slot, span, :] * SCALE2 - top).astype(bf16)
-            part = lax.dot_general(vt_ref[:, span], w, ROW_COL, preferred_element_type=f32)
+            at = block * KEY_BLOCK
+            w = jnp.exp2(s_ref[i % 2, at : at + KEY_BLOCK, :] * SCALE2 - top).astype(bf16)
+            at += half * near
+            part = lax.dot_general(
+                vt_ref[:, at : at + KEY_BLOCK], w, ROW_COL, preferred_element_type=f32
+            )
             total = part if total is None else total + part
-        message = pack(total[:HD], top, total[HD : HD + 1])
-        to = (owner & 1) * ZL + zl0
+        return total
+
+    def send(zl0, first, first_top, second, second_top):
+        top = jnp.maximum(first_top, second_top)
+        out = first * jnp.exp2(first_top - top) + second * jnp.exp2(second_top - top)
+        message = pack(out[:HD], top, out[HD : HD + 1])
+        to = to_rank * ZL + zl0
         o_ref[to] = message[:, :HD]
         o_ref[to + 1] = message[:, HD:]
 
     def run(masked):
         if own and masked:
             hide()
-        first = score(0, 0, masked)
+        tops, outs = [score(0, masked)], []
         if own:
             vt_ref[:HD, :near] = v_ref[...].astype(f32).T.astype(bf16)
             vt_ref[:HD, near:] = far_ref[:, HD:].astype(f32).T.astype(bf16)
             vt_ref[HD:, :] = jnp.ones((STAT, 2 * near), bf16)
-        second = score(2, 1, masked)
-        weigh(0, 0, first)
-        weigh(2, 1, second)
+        for i in range(len(chunks)):
+            if i + 1 < len(chunks):
+                tops.append(score(i + 1, masked))
+            outs.append(weigh(i, tops[i]))
+            if i % 2:
+                send(chunks[i][0], outs[i - 1], tops[i - 1], outs[i], tops[i])
 
     whole = (near_base + near <= cached_end) & (far_base + near <= cached_end)
     pl.when(whole)(lambda: run(False))
@@ -121,7 +139,7 @@
 def attend(info, queries, keys, values, far, earlier=None):
     own = earlier is None
     count = 2 * keys.shape[0]
-    message = jax.ShapeDtypeStruct((XB * ZL, ROWS, HD), bf16)
+    message = jax.ShapeDtypeStruct((2 * ZL, ROWS, HD), bf16)
     turned = jax.ShapeDtypeStruct((ROWS, count), bf16)
     hidden = jax.ShapeDtypeStruct((count, HD), bf16)
     operands = [info, queries, keys, values, far]
@@ -133,7 +151,7 @@
         out_shape=(message, turned, hidden) if own else message,
         in_specs=[pl.BlockSpec(memory_space=pltpu.SMEM)] + in_vmem(len(operands) - 1),
         out_specs=tuple(in_vmem(3)) if own else in_vmem(1)[0],
-        scratch_shapes=[pltpu.VMEM((2, count, 2 * HD), f32)],
+        scratch_shapes=[pltpu.VMEM((2, count // 2, 2 * HD), f32)],
         input_output_aliases={} if own else {7: 0},
         compiler_params=pltpu.CompilerParams(vmem_limit_bytes=14 * MIB),
         cost_estimate=pl.CostEstimate(
@@ -218,8 +236,10 @@
     )(rows, weight)
 
 
-def exchange(parts, axes):
-    return lax.all_to_all(parts, axes, split_axis=0, concat_axis=0, tiled=True)
+def exchange(parts, axes, groups=None):
+    return lax.all_to_all(
+        parts, axes, split_axis=0, concat_axis=0, axis_index_groups=groups, tiled=True
+    )
 
 
 def spread(part, axes, count):
@@ -228,30 +248,32 @@
 
 def per_device(queries, cache_keys, cache_values, out_weight, cached_length, start):
     count = cache_keys.shape[0]
-    x = lax.axis_index(("xa", "xb"))
+    x, c = lax.axis_index("x"), lax.axis_index("c")
     z = lax.axis_index(("zh", "zl"))
     depth = ZH * ZL
-    near_base, far_base = (x * depth + z) * count, ((3 - x) * depth + z) * count
-    info = jnp.stack([x, near_base, far_base, cached_length[0], start[0]]).astype(jnp.int32)
+    pair, far_x = jnp.where(c == 0, x ^ 1, 3 - x), jnp.where(c == 0, 3 - x, x ^ 1)
+    rank = jnp.where(c == 0, x & 1, x >> 1)
+    near_base, far_base = (x * depth + z) * count, (far_x * depth + z) * count
+    info = jnp.stack([x, pair, rank, near_base, far_base, cached_length[0], start[0]])
+    info = info.astype(jnp.int32)
     cache = jnp.concatenate([cache_keys, cache_values], axis=1)
     cache, queries = lax.optimization_barrier((cache, queries))
-    far = lax.ppermute(cache, ("xa", "xb"), [(0, 3), (3, 0), (1, 2), (2, 1)])
+    far = lax.ppermute(cache, ("c", "x"), SWAP)
     own = spread(queries.reshape(2 * GROUP, HD), ("zh", "zl"), depth)
     own = own.reshape(depth * 2 * GROUP, HD)
-    other = lax.ppermute(own, "xb", [(0, 1), (1, 0)])
+    other = lax.ppermute(own, ("c", "x"), SHARE)
     earlier = attend(info, own, cache_keys, cache_values, far)
     parts = attend(info, other, cache_keys, cache_values, far, earlier)
-    came = exchange(parts, ("xb", "zl"))
+    came = exchange(parts, ("c", "x", "zl"), OWNER_GROUPS)
     came = exchange(merge(came, ZH), ("zh",))
-    attention = exchange(finish(came, OWNERS), ("xa", "xb", "zl"))
+    attention = exchange(finish(came, OWNERS), ("x", "zl"))
     partial_out = exchange(project(attention, out_weight), ("y", "c"))
     return jnp.sum(partial_out, axis=0).astype(bf16)
 
 
 def solution(mesh):
-    shape = (4, 2, XA, XB, ZH, ZL)
-    fine = Mesh(mesh.devices.reshape(shape), ("y", "c", "xa", "xb", "zh", "zl"))
-    ctx, kv = ("xa", "xb", "zh", "zl"), ("y", "c")
+    fine = Mesh(mesh.devices.reshape(4, 2, X, ZH, ZL), ("y", "c", "x", "zh", "zl"))
+    ctx, kv = ("x", "zh", "zl"), ("y", "c")
     return jax.shard_map(
         per_device,
         mesh=fine,

time: 109 us -> 112 us (1.028)
  blocking collectives: 91.2 us -> 93.6 us
    all_to_all x5, blocking collectives: 91.2 us -> 93.6 us  [exchange(): lax.all_to_all(parts, axes, split_axis=0, concat_axis=0, axis_index_group...]
where the time goes in v7:
time: 112 us; the launch traced here: 111 us
  blocking collectives  93.6 us (84%)
  starting transfers between devices  7.68 us (7%)
  Pallas kernels  6.23 us (6%)
  other arithmetic  2.02 us (2%)
  between operations  1.41 us (1%)
    all_to_all x5, blocking collectives, exchange(): lax.all_to_all(parts, axes, split_axis=0, concat_axis=0, axis_index_group...  93.6 us
    pallas_call x2, Pallas kernels, attend(): pl.pallas_call(functools.partial(attend_kernel, own=own), out_shape=(mess...  5.66 us
    ppermute x1, starting transfers between devices, per_device(): far = lax.ppermute(cache, ('c', 'x'), SWAP)  3.95 us
    ppermute x1, starting transfers between devices, per_device(): other = lax.ppermute(own, ('c', 'x'), SHARE)  3.73 us
  transfers between devices with their start and end apart: 2, of which 0 were waited for; matrix products, arithmetic and copies ran while one was open for 0% of the time, Pallas kernels for 3%

profile of v7, /device:TPU:1, one launch (start us, length us, event | category | flops | bytes accessed | tf_op | source)
XLA Modules:
  0.0 111.1 jit_solution(202563882545125184)
XLA Ops:
  0.0 0.0 copy-start.1
  0.0 0.0 copy-start
  0.0 0.0 copy-start.3
  0.0 1.4 %pad_maximum_fusion = bf16[2048,256]{1,0:T(8,128)(2,1)S(1)} fusion(bf16[2048,128]{1,0:T(8,128)(2,1)} %v_ref.3, bf16[2048,128]{1,0:T(8,128)(2,1)} %k_ref.3), kind=kLoop, calls=%fused_computation | loop fusion | flops 2097152 | bytes 2097152 | tf_op jit(solution)/shard_map/concatenate | solution.py:259
  1.4 3.9 %collective-permute-start.1 = (bf16[2048,256]{1,0:T(8,128)(2,1)S(1)}, bf16[2048,256]{1,0:T(8,128)(2,1)S(1)}, u32[]{:S(2)}, u32[]{:S(2)}) collective-permute-start(bf16[2048,256]{1,0:T(8,128)(2,1)S(1)} %pad_maximum_fusion), channel_id=1, source_target_pairs={{0,48},{16,32},{32,16},{48,0},{64,80},{80,64},{96,112},{112,96},{1... | collective-permute-start | bytes 3145736 | tf_op jit(solution)/shard_map/ppermute | solution.py:261
  5.4 0.0 copy-done.3
  5.4 26.7 %all_to_all.25 = bf16[16,32,128]{2,1,0:T(8,128)(2,1)S(1)} all-to-all(bf16[16,32,128]{2,1,0:T(8,128)(2,1)S(1)} %broadcast_in_dim.8), channel_id=1, replica_groups=mesh['y'=4,'c'=2,'x'=4,'zh'=4,'zl'=4] {'zh','zl'}, dimensions={0} | all-to-all | bytes 262144 | tf_op jit(solution)/shard_map/all_to_all | solution.py:240
  32.1 3.7 %collective-permute-start = (bf16[512,128]{1,0:T(8,128)(2,1)S(1)}, bf16[512,128]{1,0:T(8,128)(2,1)S(1)}, u32[]{:S(2)}, u32[]{:S(2)}) collective-permute-start(bf16[512,128]{1,0:T(8,128)(2,1)S(1)} %bitcast.6), channel_id=1, source_target_pairs={{0,16},{16,0},{32,48},{48,32},{64,112},{80,96},{96,80},{112,64},{1... | collective-permute-start | bytes 393224 | tf_op jit(solution)/shard_map/ppermute | solution.py:264
  37.2 0.1 stack.23.info_ref
  37.3 0.0 collective-permute-done.1.far_ref
  37.3 0.0 copy-done.1
  37.3 0.0 copy-done
  37.3 2.8 %attend_own.1 = (bf16[8,144,128]{2,1,0:T(8,128)(2,1)S(1)}, bf16[144,4096]{1,0:T(8,128)(2,1)S(1)}, bf16[4096,128]{1,0:T(8,128)(2,1)S(1)}) custom-call(s32[7]{0:T(128)S(1)} %stack.23.info_ref, bf16[512,128]{1,0:T(8,128)(2,1)S(1)} %bitcast.7, bf16[2048,128]{1,0:T(8,128)(2,1)S(1)} %copy-done, bf16[2048,128]{1,0:T(8,128)(2,1)S(1)} %copy-done.1, ...), custom_call_target="tpu_custom_call" | custom-call | flops 1073741824 | bytes 4194304 | tf_op jit(solution)/shard_map/attend_own/pallas_call | solution.py:149
  40.1 0.0 collective-permute-done.q_ref
  40.2 2.8 %attend_other.1 = bf16[8,144,128]{2,1,0:T(8,128)(2,1)S(1)} custom-call(s32[7]{0:T(128)S(1)} %stack.23.info_ref, bf16[512,128]{1,0:T(8,128)(2,1)S(1)} %collective-permute-done.q_ref, bf16[2048,128]{1,0:T(8,128)(2,1)S(1)} %copy-done, bf16[2048,128]{1,0:T(8,128)(2,1)S(1)} %copy-done.1, ...), custom_call_target="tpu_custom_call", output_to_operand_aliasing={{}: (7, {})} | custom-call | flops 1073741824 | bytes 4194304 | tf_op jit(solution)/shard_map/attend_other/pallas_call | solution.py:149
  43.0 13.4 %all_to_all.26.in_ref = bf16[8,144,128]{2,1,0:T(8,128)(2,1)S(1)} all-to-all(bf16[8,144,128]{2,1,0:T(8,128)(2,1)S(1)} %attend_other.1), channel_id=1, replica_groups={{0,1,2,3,16,17,18,19},{32,33,34,35,48,49,50,51},{64,65,66,67,112,113,11..., dimensions={0} | all-to-all | bytes 589824 | tf_op jit(solution)/shard_map/all_to_all | solution.py:240
  56.4 0.0 copy-start.2
  56.4 0.1 merge.1
  56.5 19.2 %all_to_all.27.in_ref = bf16[4,144,128]{2,1,0:T(8,128)(2,1)S(1)} all-to-all(bf16[4,144,128]{2,1,0:T(8,128)(2,1)S(1)} %merge.1), channel_id=1, replica_groups=mesh['y'=4,'c'=2,'x'=4,'zh'=4,'zl'=4] {'zh'}, dimensions={0} | all-to-all | bytes 294912 | tf_op jit(solution)/shard_map/all_to_all | solution.py:240
  75.7 0.2 finish.1
  75.9 23.0 %all_to_all.28.a_ref = bf16[16,8,2048]{2,1,0:T(8,128)(2,1)S(1)} all-to-all(bf16[16,8,2048]{2,1,0:T(8,128)(2,1)S(1)} %finish.1), channel_id=1, replica_groups=mesh['y'=4,'c'=2,'x'=4,'zh'=4,'zl'=4] {'x','zl'}, dimensions={0} | all-to-all | bytes 1048576 | tf_op jit(solution)/shard_map/all_to_all | solution.py:240
  98.9 0.0 copy-done.2
  98.9 0.3 project.1
  99.2 11.3 %all_to_all.29 = f32[8,16,256]{2,1,0:T(8,128)S(1)} all-to-all(f32[8,16,256]{2,1,0:T(8,128)S(1)} %project.1), channel_id=1, replica_groups=mesh['y'=4,'c'=2,'x'=4,'zh'=4,'zl'=4] {'y','c'}, dimensions={0} | all-to-all | bytes 262144 | tf_op jit(solution)/shard_map/all_to_all | solution.py:240
  110.5 0.6 reduce_sum.9
  (2 shorter events, 0.0 us)
Async XLA Ops:
  0.0 37.3 %copy-start.1 = (bf16[2048,128]{1,0:T(8,128)(2,1)S(1)}, bf16[2048,128]{1,0:T(8,128)(2,1)}, u32[]{:S(2)}) copy-start(bf16[2048,128]{1,0:T(8,128)(2,1)} %v_ref.3) | copy-start | bytes 1572868
  0.0 37.3 %copy-start = (bf16[2048,128]{1,0:T(8,128)(2,1)S(1)}, bf16[2048,128]{1,0:T(8,128)(2,1)}, u32[]{:S(2)}) copy-start(bf16[2048,128]{1,0:T(8,128)(2,1)} %k_ref.3) | copy-start | bytes 1572868
  0.0 5.4 %copy-start.3 = (bf16[2,2048]{1,0:T(2,128)(2,1)S(1)}, bf16[2,2048]{1,0:T(2,128)(2,1)}, u32[]{:S(2)}) copy-start(bf16[2,2048]{1,0:T(2,128)(2,1)} %param.6) | copy-start | bytes 24580
  1.4 35.9 %collective-permute-start.1 = (bf16[2048,256]{1,0:T(8,128)(2,1)S(1)}, bf16[2048,256]{1,0:T(8,128)(2,1)S(1)}, u32[]{:S(2)}, u32[]{:S(2)}) collective-permute-start(bf16[2048,256]{1,0:T(8,128)(2,1)S(1)} %pad_maximum_fusion), channel_id=1, source_target_pairs={{0,48},{16,32},{32,16},{48,0},{64,80},{80,64},{96,112},{112,96},{1... | collective-permute-start | bytes 3145736 | tf_op jit(solution)/shard_map/ppermute | solution.py:261
  32.1 8.0 %collective-permute-start = (bf16[512,128]{1,0:T(8,128)(2,1)S(1)}, bf16[512,128]{1,0:T(8,128)(2,1)S(1)}, u32[]{:S(2)}, u32[]{:S(2)}) collective-permute-start(bf16[512,128]{1,0:T(8,128)(2,1)S(1)} %bitcast.6), channel_id=1, source_target_pairs={{0,16},{16,0},{32,48},{48,32},{64,112},{80,96},{96,80},{112,64},{1... | collective-permute-start | bytes 393224 | tf_op jit(solution)/shard_map/ppermute | solution.py:264
  56.4 42.5 %copy-start.2 = (bf16[2048,256]{1,0:T(8,128)(2,1)S(1)}, bf16[2048,256]{1,0:T(8,128)(2,1)}, u32[]{:S(2)}) copy-start(bf16[2048,256]{1,0:T(8,128)(2,1)} %w_ref.1) | copy-start | bytes 3145732

commit v8 on v4

--- a/solution.py
+++ b/solution.py
@@ -32,13 +32,21 @@
     blank = jnp.zeros((STAT - 3, out.shape[1]), f32)
     return jnp.concatenate([out, top, high, total - high, blank], axis=0).astype(bf16)
 
-def attend_kernel(info_ref, qa_ref, qb_ref, k_ref, v_ref, kv_ref, o_ref, vt_ref, s_ref, hide_ref):
-    near = k_ref.shape[0]
+def ctx_x():
+    return lax.axis_index("xa") * XB + lax.axis_index("xb")
+
+
+def attend_kernel(
+    cached_ref, start_ref, qa_ref, qb_ref, near_ref, far_ref, o_ref, vt_ref, s_ref, hide_ref
+):
+    near = near_ref.shape[0]
     keys = 2 * near
-    blocks = keys // KEY_BLOCK
-    x, near_base, far_base, cached_end, span_start = [info_ref[i] for i in range(5)]
-    vt_ref[:HD, :near] = v_ref[...].astype(f32).T.astype(bf16)
-    vt_ref[:HD, near:] = kv_ref[:, HD:].astype(f32).T.astype(bf16)
+    blocks = near // KEY_BLOCK
+    x, z = ctx_x(), lax.axis_index("zh") * ZL + lax.axis_index("zl")
+    near_base, far_base = (x * ZH * ZL + z) * near, ((3 - x) * ZH * ZL + z) * near
+    cached_end, span_start = cached_ref[0], start_ref[0]
+    vt_ref[:HD, :near] = near_ref[:, HD:].astype(f32).T.astype(bf16)
+    vt_ref[:HD, near:] = far_ref[:, HD:].astype(f32).T.astype(bf16)
     vt_ref[HD:, :] = jnp.ones((STAT, keys), bf16)
 
     def query_rows(zl):
@@ -53,8 +61,8 @@
     def key_rows(block):
         at = block * KEY_BLOCK
         if at < near:
-            return k_ref[at : at + KEY_BLOCK, :]
-        return kv_ref[at - near : at - near + KEY_BLOCK, :HD]
+            return near_ref[at : at + KEY_BLOCK, :HD]
+        return far_ref[at - near : at - near + KEY_BLOCK, :HD]
 
     def hide():
         for half, base in ((0, near_base), (1, far_base)):
@@ -70,17 +78,18 @@
         return jnp.where(owner * 32 + zh * 8 + zl * 2 + t == col, 1.0, 0.0).astype(bf16)
 
     def score(i, masked):
-        rows = query_rows(i)
+        zl, half = divmod(i, 2)
+        rows = query_rows(zl)
         if masked:
-            rows = jnp.concatenate([rows, token_rows(i)], axis=1)
+            rows = jnp.concatenate([rows, token_rows(zl)], axis=1)
         top = None
         for block in range(blocks):
-            span = slice(block * KEY_BLOCK, (block + 1) * KEY_BLOCK)
-            left = key_rows(block)
+            at = half * near + block * KEY_BLOCK
+            left = key_rows(at // KEY_BLOCK)
             if masked:
-                left = jnp.concatenate([left, hide_ref[span, :]], axis=1)
+                left = jnp.concatenate([left, hide_ref[at : at + KEY_BLOCK, :]], axis=1)
             s = lax.dot_general(left, rows, ROW_ROW, preferred_element_type=f32)
-            s_ref[i % 2, span, :] = s
+            s_ref[i % 2, block * KEY_BLOCK : (block + 1) * KEY_BLOCK, :] = s
             here = jnp.max(s.reshape(KEY_BLOCK // 8, 8, s.shape[1]), axis=0)
             top = here if top is None else jnp.maximum(top, here)
         top = jnp.max(top, axis=0, keepdims=True) * SCALE2
@@ -89,41 +98,52 @@
     def weigh(i, top):
         total = None
         for block in range(blocks):
-            span = slice(block * KEY_BLOCK, (block + 1) * KEY_BLOCK)
-            w = jnp.exp2(s_ref[i % 2, span, :] * SCALE2 - top).astype(bf16)
-            part = lax.dot_general(vt_ref[:, span], w, ROW_COL, preferred_element_type=f32)
+            at = block * KEY_BLOCK
+            w = jnp.exp2(s_ref[i % 2, at : at + KEY_BLOCK, :] * SCALE2 - top).astype(bf16)
+            at += i % 2 * near
+            part = lax.dot_general(
+                vt_ref[:, at : at + KEY_BLOCK], w, ROW_COL, preferred_element_type=f32
+            )
             total = part if total is None else total + part
-        message = pack(total[:HD], top, total[HD : HD + 1])
-        o_ref[i] = message[:, :HD]
-        o_ref[ZL + i] = message[:, HD:]
+        return total
+
+    def send(zl, first, first_top, second, second_top):
+        top = jnp.maximum(first_top, second_top)
+        out = first * jnp.exp2(first_top - top) + second * jnp.exp2(second_top - top)
+        message = pack(out[:HD], top, out[HD : HD + 1])
+        o_ref[zl] = message[:, :HD]
+        o_ref[ZL + zl] = message[:, HD:]
 
     def run(masked):
         if masked:
             hide()
-        top = score(0, masked)
-        for i in range(ZL):
-            following = score(i + 1, masked) if i + 1 < ZL else None
-            weigh(i, top)
-            top = following
+        tops, outs = [score(0, masked)], []
+        for i in range(2 * ZL):
+            if i + 1 < 2 * ZL:
+                tops.append(score(i + 1, masked))
+            outs.append(weigh(i, tops[i]))
+            if i % 2:
+                send(i // 2, outs[i - 1], tops[i - 1], outs[i], tops[i])
+
     whole = (near_base + near <= cached_end) & (far_base + near <= cached_end)
     pl.when(whole)(lambda: run(False))
     pl.when(jnp.logical_not(whole))(lambda: run(True))
 
-def attend(info, qa, qb, keys, values, far):
-    count = 2 * keys.shape[0]
+def attend(cached_length, start, qa, qb, near, far):
+    count = 2 * near.shape[0]
     return pl.pallas_call(
         attend_kernel,
         out_shape=jax.ShapeDtypeStruct((XB * ZL, ROWS, HD), bf16),
-        in_specs=[pl.BlockSpec(memory_space=pltpu.SMEM)] + in_vmem(5),
+        in_specs=[pl.BlockSpec(memory_space=pltpu.SMEM)] * 2 + in_vmem(4),
         out_specs=pl.BlockSpec(memory_space=pltpu.VMEM),
         scratch_shapes=[
             pltpu.VMEM((ROWS, count), bf16),
-            pltpu.VMEM((2, count, 2 * HD), f32),
+            pltpu.VMEM((2, count // 2, 2 * HD), f32),
             pltpu.VMEM((count, HD), bf16),
         ],
         compiler_params=pltpu.CompilerParams(vmem_limit_bytes=14 * MIB),
         name="attend",
-    )(info, qa, qb, keys, values, far)
+    )(cached_length, start, qa, qb, near, far)
 
 def merged(messages):
     tops = [m[HD : HD + 1] for m in messages]
@@ -178,9 +198,9 @@
         name="finish",
     )(came)
 
-def project_kernel(info_ref, a_ref, own_ref, other_ref, o_ref):
+def project_kernel(a_ref, own_ref, other_ref, o_ref):
     senders, tokens, depth = a_ref.shape
-    xb = info_ref[0] & 1
+    xb = lax.axis_index("xb")
     rows = a_ref[...].astype(f32).reshape(senders * tokens, depth).astype(bf16)
     for to, w_ref in ((xb, own_ref), (1 - xb, other_ref)):
         out = jnp.dot(rows, w_ref[...], preferred_element_type=f32)
@@ -193,15 +213,15 @@
                 o_ref[(x * 2 + half) * XB + to] = jnp.concatenate(parts, axis=0)
 
 
-def project(info, rows, weight, other):
+def project(rows, weight, other):
     return pl.pallas_call(
         project_kernel,
         out_shape=jax.ShapeDtypeStruct((8 * XB, 8, weight.shape[1]), f32),
-        in_specs=[pl.BlockSpec(memory_space=pltpu.SMEM)] + in_vmem(3),
+        in_specs=in_vmem(3),
         out_specs=pl.BlockSpec(memory_space=pltpu.VMEM),
         compiler_params=pltpu.CompilerParams(vmem_limit_bytes=8 * MIB),
         name="project",
-    )(info, rows, weight, other)
+    )(rows, weight, other)
 
 
 def total_kernel(in_ref, o_ref, s_ref):
@@ -233,31 +253,20 @@
     return lax.all_to_all(parts, axes, split_axis=0, concat_axis=0, tiled=True)
 
 
-def spread(part, axes, count):
-    return exchange(jnp.broadcast_to(part[None], (count,) + part.shape), axes)
-
-
 def per_device(queries, cache_keys, cache_values, out_weight, cached_length, start):
-    count = cache_keys.shape[0]
-    x = lax.axis_index(("xa", "xb"))
-    z = lax.axis_index(("zh", "zl"))
-    depth = ZH * ZL
-    near_base, far_base = (x * depth + z) * count, ((3 - x) * depth + z) * count
-    info = jnp.stack([x, near_base, far_base, cached_length[0], start[0]]).astype(jnp.int32)
-    cache = jnp.concatenate([cache_keys, cache_values], axis=1)
-    cache, queries = lax.optimization_barrier((cache, queries))
-    far = lax.ppermute(cache, ("xa", "xb"), [(0, 3), (3, 0), (1, 2), (2, 1)])
-    own = spread(queries.reshape(2 * GROUP, HD), ("zh", "zl"), depth)
-    own = own.reshape(depth * 2 * GROUP, HD)
     swap = [(0, 1), (1, 0)]
+    near = jnp.concatenate([cache_keys, cache_values], axis=1)
+    near, queries = lax.optimization_barrier((near, queries))
+    rows = jnp.broadcast_to(queries.reshape(1, 2 * GROUP, HD), (ZH * ZL, 2 * GROUP, HD))
+    far = lax.ppermute(near, ("xa", "xb"), [(0, 3), (3, 0), (1, 2), (2, 1)])
+    own = exchange(rows, ("zh", "zl")).reshape(ZH * ZL * 2 * GROUP, HD)
     other = lax.ppermute(own, "xb", swap)
     other_weight = lax.ppermute(out_weight, "xb", swap)
-    parts = attend(info, own, other, cache_keys, cache_values, far)
-    came = exchange(parts, ("xb", "zl"))
+    came = exchange(attend(cached_length, start, own, other, near, far), ("xb", "zl"))
     came = exchange(merge(came, ZH), ("zh",))
-    attention = exchange(finish(came, XA * ZL), ("xa", "zl"))
-    partial_out = exchange(project(info, attention, out_weight, other_weight), ("y", "c", "xb"))
-    return total(partial_out)
+    done, other_weight = lax.optimization_barrier((finish(came, XA * ZL), other_weight))
+    attention = exchange(done, ("xa", "zl"))
+    return total(exchange(project(attention, out_weight, other_weight), ("y", "c", "xb")))
 
 
 def solution(mesh):

time: 109 us -> 106 us (0.972)
  blocking collectives: 55.3 us -> 74.7 us
  waiting for transfers between devices: 21.5 us -> 7.36 us
  starting transfers between devices: 20.6 us -> 14.4 us
  Pallas kernels: 8.33 us -> 6.39 us
    all_to_all x3 -> x4, blocking collectives: 55.3 us -> 74.7 us  [exchange(): return lax.all_to_all(parts, axes, split_axis=0, concat_axis=0, tiled=True)]
    all_to_all x2 -> x1, waiting for transfers between devices: 16.3 us -> 4.42 us  [exchange(): return lax.all_to_all(parts, axes, split_axis=0, concat_axis=0, tiled=True)]
    all_to_all x2 -> x1, starting transfers between devices: 11.3 us -> 3.96 us  [exchange(): return lax.all_to_all(parts, axes, split_axis=0, concat_axis=0, tiled=True)]
    ppermute x1, waiting for transfers between devices: 2.85 us -> 0.46 us  [per_device(): other_weight = lax.ppermute(out_weight, 'xb', swap)]
    ppermute x1, starting transfers between devices: 2.18 us -> 3.36 us  [per_device(): other_weight = lax.ppermute(out_weight, 'xb', swap)]
  transfers between devices with their start and end apart: 5 -> 4, of which waited for: 4 -> 3; matrix products, arithmetic and copies ran while one was open for 0% -> 0% of each run, Pallas kernels for 1% -> 0%
where the time goes in v8:
time: 106 us
  blocking collectives  74.7 us (70%)
  starting transfers between devices  14.4 us (14%)
  waiting for transfers between devices  7.36 us (7%)
  Pallas kernels  6.39 us (6%)
  between operations  1.38 us (1%)
  other arithmetic  1.33 us (1%)
    all_to_all x4, blocking collectives, exchange(): return lax.all_to_all(parts, axes, split_axis=0, concat_axis=0, tiled=True)  74.7 us
    ppermute x1, starting transfers between devices, per_device(): far = lax.ppermute(near, ('xa', 'xb'), [(0, 3), (3, 0), (1, 2), (2, 1)])  5.22 us
    pallas_call x1, Pallas kernels, attend(): pl.pallas_call(attend_kernel, out_shape=jax.ShapeDtypeStruct((XB * ZL, RO...  4.99 us
    all_to_all x1, waiting for transfers between devices, exchange(): return lax.all_to_all(parts, axes, split_axis=0, concat_axis=0, tiled=True)  4.42 us
    all_to_all x1, starting transfers between devices, exchange(): return lax.all_to_all(parts, axes, split_axis=0, concat_axis=0, tiled=True)  3.96 us
    ppermute x1, starting transfers between devices, per_device(): other_weight = lax.ppermute(out_weight, 'xb', swap)  3.36 us
    ppermute x1, waiting for transfers between devices, per_device(): other = lax.ppermute(own, 'xb', swap)  2.48 us
  transfers between devices with their start and end apart: 4, of which 3 were waited for; matrix products, arithmetic and copies ran while one was open for 0% of the time, Pallas kernels for 0%

profile of v8, /device:TPU:1, one launch (start us, length us, event | category | flops | bytes accessed | tf_op | source)
XLA Modules:
  0.0 105.6 jit_solution(7431644732185175899)
XLA Ops:
  0.0 0.0 copy-start.1
  0.0 1.3 %pad_maximum_fusion.near_ref = bf16[2048,256]{1,0:T(8,128)(2,1)S(1)} fusion(bf16[2048,128]{1,0:T(8,128)(2,1)} %param.8, bf16[2048,128]{1,0:T(8,128)(2,1)} %param.7), kind=kLoop, calls=%fused_computation | loop fusion | flops 2097152 | bytes 2097152 | tf_op jit(solution)/shard_map/concatenate | solution.py:258
  1.3 5.2 %collective-permute-start.1 = (bf16[2048,256]{1,0:T(8,128)(2,1)S(1)}, bf16[2048,256]{1,0:T(8,128)(2,1)S(1)}, u32[]{:S(2)}, u32[]{:S(2)}) collective-permute-start(bf16[2048,256]{1,0:T(8,128)(2,1)S(1)} %pad_maximum_fusion.near_ref), channel_id=1, source_target_pairs={{0,48},{48,0},{16,32},{32,16},{1,49},{49,1},{17,33},{33,17},{2,50}... | collective-permute-start | bytes 3145736 | tf_op jit(solution)/shard_map/ppermute | solution.py:261
  6.6 0.0 copy-done.1
  6.6 26.7 %all_to_all.25 = bf16[16,32,128]{2,1,0:T(8,128)(2,1)S(1)} all-to-all(bf16[16,32,128]{2,1,0:T(8,128)(2,1)S(1)} %broadcast_in_dim.8), channel_id=1, replica_groups=mesh['y'=4,'c'=2,'xa'=2,'xb'=2,'zh'=4,'zl'=4] {'zh','zl'}, dimensions={0} | all-to-all | bytes 262144 | tf_op jit(solution)/shard_map/all_to_all | solution.py:253
  33.3 1.9 %collective-permute-start = (bf16[512,128]{1,0:T(8,128)(2,1)S(1)}, bf16[512,128]{1,0:T(8,128)(2,1)S(1)}, u32[]{:S(2)}, u32[]{:S(2)}) collective-permute-start(bf16[512,128]{1,0:T(8,128)(2,1)S(1)} %bitcast.1), channel_id=1, source_target_pairs={{0,16},{16,0},{1,17},{17,1},{2,18},{18,2},{3,19},{19,3},{4,20},{20... | collective-permute-start | bytes 393224 | tf_op jit(solution)/shard_map/ppermute | solution.py:263
  36.5 0.0 copy-start
  36.5 2.5 %collective-permute-done.qb_ref = bf16[512,128]{1,0:T(8,128)(2,1)S(1)} collective-permute-done((bf16[512,128]{1,0:T(8,128)(2,1)S(1)}, bf16[512,128]{1,0:T(8,128)(2,1)S(1)}, u32[]{:S(2)}, u32[]{:S(2)}) %collective-permute-start) | collective-permute-done | bytes 131104 | tf_op jit(solution)/shard_map/ppermute | solution.py:263
  39.0 0.0 collective-permute-done.1.far_ref
  39.0 5.0 %attend.1 = bf16[8,144,128]{2,1,0:T(8,128)(2,1)} custom-call(s32[1]{0:T(128)S(6)} %copy.7.cached_ref, s32[1]{0:T(128)S(6)} %copy.8.start_ref, bf16[512,128]{1,0:T(8,128)(2,1)S(1)} %bitcast.2, bf16[512,128]{1,0:T(8,128)(2,1)S(1)} %collective-permute-done.qb_ref, bf16[2048,256]{1,0:T(8,128)(2,1)S(1)} %pad_maximum_fusion.near_ref, ...), custom_call_target="tpu_custom_call" | custom-call | tf_op jit(solution)/shard_map/attend/pallas_call | solution.py:134
  44.0 4.0 %all-to-all-start.1 = ((bf16[8,144,128]{2,1,0:T(8,128)(2,1)}), bf16[8,144,128]{2,1,0:T(8,128)(2,1)S(1)}, u32[]{:S(2)}, u32[]{:S(2)}) async-start(bf16[8,144,128]{2,1,0:T(8,128)(2,1)} %attend.1), calls=%async_computation.1 | async-start | bytes 589824 | tf_op jit(solution)/shard_map/all_to_all | solution.py:253
  48.0 0.0 copy-done
  48.0 3.4 %collective-permute-start.2 = (bf16[2048,256]{1,0:T(8,128)(2,1)S(1)}, bf16[2048,256]{1,0:T(8,128)(2,1)S(1)}, u32[]{:S(2)}, u32[]{:S(2)}) collective-permute-start(bf16[2048,256]{1,0:T(8,128)(2,1)S(1)} %copy-done), channel_id=1, source_target_pairs={{0,16},{16,0},{1,17},{17,1},{2,18},{18,2},{3,19},{19,3},{4,20},{20... | collective-permute-start | bytes 3145736 | tf_op jit(solution)/shard_map/ppermute | solution.py:264
  51.3 4.4 %all-to-all-done.1.in_ref = bf16[8,144,128]{2,1,0:T(8,128)(2,1)S(1)} async-done(((bf16[8,144,128]{2,1,0:T(8,128)(2,1)}), bf16[8,144,128]{2,1,0:T(8,128)(2,1)S(1)}, u32[]{:S(2)}, u32[]{:S(2)}) %all-to-all-start.1) | async-done | bytes 294944 | tf_op jit(solution)/shard_map/all_to_all | solution.py:253
  55.8 0.1 merge.1
  55.9 17.8 %all_to_all.26.in_ref = bf16[4,144,128]{2,1,0:T(8,128)(2,1)S(1)} all-to-all(bf16[4,144,128]{2,1,0:T(8,128)(2,1)S(1)} %merge.1), channel_id=1, replica_groups=mesh['y'=4,'c'=2,'xa'=2,'xb'=2,'zh'=4,'zl'=4] {'zh'}, dimensions={0} | all-to-all | bytes 294912 | tf_op jit(solution)/shard_map/all_to_all | solution.py:253
  73.7 0.1 finish.1
  73.9 0.5 collective-permute-done.2.other_ref
  74.3 13.4 %all_to_all.27.a_ref = bf16[8,8,2048]{2,1,0:T(8,128)(2,1)S(1)} all-to-all(bf16[8,8,2048]{2,1,0:T(8,128)(2,1)S(1)} %finish.1), channel_id=1, replica_groups=mesh['y'=4,'c'=2,'xa'=2,'xb'=2,'zh'=4,'zl'=4] {'xa','zl'}, dimensions={0} | all-to-all | bytes 524288 | tf_op jit(solution)/shard_map/all_to_all | solution.py:253
  87.8 0.5 project.1
  88.3 16.7 %all_to_all.28.in_ref = f32[16,8,256]{2,1,0:T(8,128)S(1)} all-to-all(f32[16,8,256]{2,1,0:T(8,128)S(1)} %project.1), channel_id=1, replica_groups=mesh['y'=4,'c'=2,'xa'=2,'xb'=2,'zh'=4,'zl'=4] {'y','c','xb'}, dimensions={0} | all-to-all | bytes 262144 | tf_op jit(solution)/shard_map/all_to_all | solution.py:253
  105.0 0.6 total.1
  (2 shorter events, 0.0 us)
Async XLA Ops:
  0.0 6.6 %copy-start.1 = (bf16[2,2048]{1,0:T(2,128)(2,1)S(1)}, bf16[2,2048]{1,0:T(2,128)(2,1)}, u32[]{:S(2)}) copy-start(bf16[2,2048]{1,0:T(2,128)(2,1)} %param.6) | copy-start | bytes 24580
  1.3 37.7 %collective-permute-start.1 = (bf16[2048,256]{1,0:T(8,128)(2,1)S(1)}, bf16[2048,256]{1,0:T(8,128)(2,1)S(1)}, u32[]{:S(2)}, u32[]{:S(2)}) collective-permute-start(bf16[2048,256]{1,0:T(8,128)(2,1)S(1)} %pad_maximum_fusion.near_ref), channel_id=1, source_target_pairs={{0,48},{48,0},{16,32},{32,16},{1,49},{49,1},{17,33},{33,17},{2,50}... | collective-permute-start | bytes 3145736 | tf_op jit(solution)/shard_map/ppermute | solution.py:261
  33.3 5.7 %collective-permute-start = (bf16[512,128]{1,0:T(8,128)(2,1)S(1)}, bf16[512,128]{1,0:T(8,128)(2,1)S(1)}, u32[]{:S(2)}, u32[]{:S(2)}) collective-permute-start(bf16[512,128]{1,0:T(8,128)(2,1)S(1)} %bitcast.1), channel_id=1, source_target_pairs={{0,16},{16,0},{1,17},{17,1},{2,18},{18,2},{3,19},{19,3},{4,20},{20... | collective-permute-start | bytes 393224 | tf_op jit(solution)/shard_map/ppermute | solution.py:263
  36.5 11.4 %copy-start = (bf16[2048,256]{1,0:T(8,128)(2,1)S(1)}, bf16[2048,256]{1,0:T(8,128)(2,1)}, u32[]{:S(2)}) copy-start(bf16[2048,256]{1,0:T(8,128)(2,1)} %own_ref.1) | copy-start | bytes 3145732
  44.0 11.8 %all-to-all-start.1 = ((bf16[8,144,128]{2,1,0:T(8,128)(2,1)}), bf16[8,144,128]{2,1,0:T(8,128)(2,1)S(1)}, u32[]{:S(2)}, u32[]{:S(2)}) async-start(bf16[8,144,128]{2,1,0:T(8,128)(2,1)} %attend.1), calls=%async_computation.1 | async-start | bytes 589824 | tf_op jit(solution)/shard_map/all_to_all | solution.py:253
  48.0 26.4 %collective-permute-start.2 = (bf16[2048,256]{1,0:T(8,128)(2,1)S(1)}, bf16[2048,256]{1,0:T(8,128)(2,1)S(1)}, u32[]{:S(2)}, u32[]{:S(2)}) collective-permute-start(bf16[2048,256]{1,0:T(8,128)(2,1)S(1)} %copy-done), channel_id=1, source_target_pairs={{0,16},{16,0},{1,17},{17,1},{2,18},{18,2},{3,19},{19,3},{4,20},{20... | collective-permute-start | bytes 3145736 | tf_op jit(solution)/shard_map/ppermute | solution.py:264

commit v9 on v8

--- a/solution.py
+++ b/solution.py
@@ -12,7 +12,8 @@
 GROUP = 16
 SCALE2 = math.log2(math.e) / math.sqrt(HD)
 XA, XB, ZH, ZL = 2, 2, 4, 4
-STAT = 16
+STAT = 8
+ONES = 16
 ROWS = HD + STAT
 KEY_BLOCK = 256
 HIDDEN = -1e30
@@ -45,9 +46,6 @@
     x, z = ctx_x(), lax.axis_index("zh") * ZL + lax.axis_index("zl")
     near_base, far_base = (x * ZH * ZL + z) * near, ((3 - x) * ZH * ZL + z) * near
     cached_end, span_start = cached_ref[0], start_ref[0]
-    vt_ref[:HD, :near] = near_ref[:, HD:].astype(f32).T.astype(bf16)
-    vt_ref[:HD, near:] = far_ref[:, HD:].astype(f32).T.astype(bf16)
-    vt_ref[HD:, :] = jnp.ones((STAT, keys), bf16)
 
     def query_rows(zl):
         parts = []
@@ -118,6 +116,9 @@
         if masked:
             hide()
         tops, outs = [score(0, masked)], []
+        vt_ref[:HD, :near] = near_ref[:, HD:].astype(f32).T.astype(bf16)
+        vt_ref[:HD, near:] = far_ref[:, HD:].astype(f32).T.astype(bf16)
+        vt_ref[HD:, :] = jnp.ones((ONES, keys), bf16)
         for i in range(2 * ZL):
             if i + 1 < 2 * ZL:
                 tops.append(score(i + 1, masked))
@@ -137,7 +138,7 @@
         in_specs=[pl.BlockSpec(memory_space=pltpu.SMEM)] * 2 + in_vmem(4),
         out_specs=pl.BlockSpec(memory_space=pltpu.VMEM),
         scratch_shapes=[
-            pltpu.VMEM((ROWS, count), bf16),
+            pltpu.VMEM((HD + ONES, count), bf16),
             pltpu.VMEM((2, count // 2, 2 * HD), f32),
             pltpu.VMEM((count, HD), bf16),
         ],

time: 106 us -> 105 us (level)
  no operation moved by 1% of the time
where the time goes in v9:
time: 105 us
  blocking collectives  74.6 us (71%)
  starting transfers between devices  14.4 us (14%)
  waiting for transfers between devices  7.17 us (7%)
  Pallas kernels  6.1 us (6%)
  between operations  1.38 us (1%)
  other arithmetic  1.33 us (1%)
    all_to_all x4, blocking collectives, exchange(): return lax.all_to_all(parts, axes, split_axis=0, concat_axis=0, tiled=True)  74.6 us
    ppermute x1, starting transfers between devices, per_device(): far = lax.ppermute(near, ('xa', 'xb'), [(0, 3), (3, 0), (1, 2), (2, 1)])  5.22 us
    pallas_call x1, Pallas kernels, attend(): pl.pallas_call(attend_kernel, out_shape=jax.ShapeDtypeStruct((XB * ZL, RO...  4.7 us
    all_to_all x1, waiting for transfers between devices, exchange(): return lax.all_to_all(parts, axes, split_axis=0, concat_axis=0, tiled=True)  4.29 us
    all_to_all x1, starting transfers between devices, exchange(): return lax.all_to_all(parts, axes, split_axis=0, concat_axis=0, tiled=True)  3.95 us
    ppermute x1, starting transfers between devices, per_device(): other_weight = lax.ppermute(out_weight, 'xb', swap)  3.36 us
    ppermute x1, waiting for transfers between devices, per_device(): other = lax.ppermute(own, 'xb', swap)  2.48 us
  transfers between devices with their start and end apart: 4, of which 3 were waited for; matrix products, arithmetic and copies ran while one was open for 0% of the time, Pallas kernels for 0%

profile of v9, /device:TPU:1, one launch (start us, length us, event | category | flops | bytes accessed | tf_op | source)
XLA Modules:
  0.0 105.0 jit_solution(13805216432533222013)
XLA Ops:
  0.0 0.0 copy-start.1
  0.0 1.3 %pad_maximum_fusion.near_ref = bf16[2048,256]{1,0:T(8,128)(2,1)S(1)} fusion(bf16[2048,128]{1,0:T(8,128)(2,1)} %param.8, bf16[2048,128]{1,0:T(8,128)(2,1)} %param.7), kind=kLoop, calls=%fused_computation | loop fusion | flops 2097152 | bytes 2097152 | tf_op jit(solution)/shard_map/concatenate | solution.py:259
  1.3 5.2 %collective-permute-start.1 = (bf16[2048,256]{1,0:T(8,128)(2,1)S(1)}, bf16[2048,256]{1,0:T(8,128)(2,1)S(1)}, u32[]{:S(2)}, u32[]{:S(2)}) collective-permute-start(bf16[2048,256]{1,0:T(8,128)(2,1)S(1)} %pad_maximum_fusion.near_ref), channel_id=1, source_target_pairs={{0,48},{48,0},{16,32},{32,16},{1,49},{49,1},{17,33},{33,17},{2,50}... | collective-permute-start | bytes 3145736 | tf_op jit(solution)/shard_map/ppermute | solution.py:262
  6.6 0.0 copy-done.1
  6.6 26.7 %all_to_all.25 = bf16[16,32,128]{2,1,0:T(8,128)(2,1)S(1)} all-to-all(bf16[16,32,128]{2,1,0:T(8,128)(2,1)S(1)} %broadcast_in_dim.8), channel_id=1, replica_groups=mesh['y'=4,'c'=2,'xa'=2,'xb'=2,'zh'=4,'zl'=4] {'zh','zl'}, dimensions={0} | all-to-all | bytes 262144 | tf_op jit(solution)/shard_map/all_to_all | solution.py:254
  33.3 1.9 %collective-permute-start = (bf16[512,128]{1,0:T(8,128)(2,1)S(1)}, bf16[512,128]{1,0:T(8,128)(2,1)S(1)}, u32[]{:S(2)}, u32[]{:S(2)}) collective-permute-start(bf16[512,128]{1,0:T(8,128)(2,1)S(1)} %bitcast.1), channel_id=1, source_target_pairs={{0,16},{16,0},{1,17},{17,1},{2,18},{18,2},{3,19},{19,3},{4,20},{20... | collective-permute-start | bytes 393224 | tf_op jit(solution)/shard_map/ppermute | solution.py:264
  36.5 0.0 copy-start
  36.5 2.5 %collective-permute-done.qb_ref = bf16[512,128]{1,0:T(8,128)(2,1)S(1)} collective-permute-done((bf16[512,128]{1,0:T(8,128)(2,1)S(1)}, bf16[512,128]{1,0:T(8,128)(2,1)S(1)}, u32[]{:S(2)}, u32[]{:S(2)}) %collective-permute-start) | collective-permute-done | bytes 131104 | tf_op jit(solution)/shard_map/ppermute | solution.py:264
  39.0 0.0 collective-permute-done.1.far_ref
  39.0 4.7 %attend.1 = bf16[8,136,128]{2,1,0:T(8,128)(2,1)} custom-call(s32[1]{0:T(128)S(6)} %copy.7.cached_ref, s32[1]{0:T(128)S(6)} %copy.8.start_ref, bf16[512,128]{1,0:T(8,128)(2,1)S(1)} %bitcast.2, bf16[512,128]{1,0:T(8,128)(2,1)S(1)} %collective-permute-done.qb_ref, bf16[2048,256]{1,0:T(8,128)(2,1)S(1)} %pad_maximum_fusion.near_ref, ...), custom_call_target="tpu_custom_call" | custom-call | tf_op jit(solution)/shard_map/attend/pallas_call | solution.py:135
  43.7 3.9 %all-to-all-start.1 = ((bf16[8,136,128]{2,1,0:T(8,128)(2,1)}), bf16[8,136,128]{2,1,0:T(8,128)(2,1)S(1)}, u32[]{:S(2)}, u32[]{:S(2)}) async-start(bf16[8,136,128]{2,1,0:T(8,128)(2,1)} %attend.1), calls=%async_computation.1 | async-start | bytes 557056 | tf_op jit(solution)/shard_map/all_to_all | solution.py:254
  47.7 0.0 copy-done
  47.7 3.4 %collective-permute-start.2 = (bf16[2048,256]{1,0:T(8,128)(2,1)S(1)}, bf16[2048,256]{1,0:T(8,128)(2,1)S(1)}, u32[]{:S(2)}, u32[]{:S(2)}) collective-permute-start(bf16[2048,256]{1,0:T(8,128)(2,1)S(1)} %copy-done), channel_id=1, source_target_pairs={{0,16},{16,0},{1,17},{17,1},{2,18},{18,2},{3,19},{19,3},{4,20},{20... | collective-permute-start | bytes 3145736 | tf_op jit(solution)/shard_map/ppermute | solution.py:265
  51.0 4.3 %all-to-all-done.1.in_ref = bf16[8,136,128]{2,1,0:T(8,128)(2,1)S(1)} async-done(((bf16[8,136,128]{2,1,0:T(8,128)(2,1)}), bf16[8,136,128]{2,1,0:T(8,128)(2,1)S(1)}, u32[]{:S(2)}, u32[]{:S(2)}) %all-to-all-start.1) | async-done | bytes 278560 | tf_op jit(solution)/shard_map/all_to_all | solution.py:254
  55.3 0.1 merge.1
  55.5 17.8 %all_to_all.26.in_ref = bf16[4,136,128]{2,1,0:T(8,128)(2,1)S(1)} all-to-all(bf16[4,136,128]{2,1,0:T(8,128)(2,1)S(1)} %merge.1), channel_id=1, replica_groups=mesh['y'=4,'c'=2,'xa'=2,'xb'=2,'zh'=4,'zl'=4] {'zh'}, dimensions={0} | all-to-all | bytes 278528 | tf_op jit(solution)/shard_map/all_to_all | solution.py:254
  73.3 0.1 finish.1
  73.4 0.4 collective-permute-done.2.other_ref
  73.8 13.2 %all_to_all.27.a_ref = bf16[8,8,2048]{2,1,0:T(8,128)(2,1)S(1)} all-to-all(bf16[8,8,2048]{2,1,0:T(8,128)(2,1)S(1)} %finish.1), channel_id=1, replica_groups=mesh['y'=4,'c'=2,'xa'=2,'xb'=2,'zh'=4,'zl'=4] {'xa','zl'}, dimensions={0} | all-to-all | bytes 524288 | tf_op jit(solution)/shard_map/all_to_all | solution.py:254
  87.0 0.5 project.1
  87.5 16.9 %all_to_all.28.in_ref = f32[16,8,256]{2,1,0:T(8,128)S(1)} all-to-all(f32[16,8,256]{2,1,0:T(8,128)S(1)} %project.1), channel_id=1, replica_groups=mesh['y'=4,'c'=2,'xa'=2,'xb'=2,'zh'=4,'zl'=4] {'y','c','xb'}, dimensions={0} | all-to-all | bytes 262144 | tf_op jit(solution)/shard_map/all_to_all | solution.py:254
  104.4 0.6 total.1
  (2 shorter events, 0.0 us)
Async XLA Ops:
  0.0 6.6 %copy-start.1 = (bf16[2,2048]{1,0:T(2,128)(2,1)S(1)}, bf16[2,2048]{1,0:T(2,128)(2,1)}, u32[]{:S(2)}) copy-start(bf16[2,2048]{1,0:T(2,128)(2,1)} %param.6) | copy-start | bytes 24580
  1.3 37.7 %collective-permute-start.1 = (bf16[2048,256]{1,0:T(8,128)(2,1)S(1)}, bf16[2048,256]{1,0:T(8,128)(2,1)S(1)}, u32[]{:S(2)}, u32[]{:S(2)}) collective-permute-start(bf16[2048,256]{1,0:T(8,128)(2,1)S(1)} %pad_maximum_fusion.near_ref), channel_id=1, source_target_pairs={{0,48},{48,0},{16,32},{32,16},{1,49},{49,1},{17,33},{33,17},{2,50}... | collective-permute-start | bytes 3145736 | tf_op jit(solution)/shard_map/ppermute | solution.py:262
  33.3 5.7 %collective-permute-start = (bf16[512,128]{1,0:T(8,128)(2,1)S(1)}, bf16[512,128]{1,0:T(8,128)(2,1)S(1)}, u32[]{:S(2)}, u32[]{:S(2)}) collective-permute-start(bf16[512,128]{1,0:T(8,128)(2,1)S(1)} %bitcast.1), channel_id=1, source_target_pairs={{0,16},{16,0},{1,17},{17,1},{2,18},{18,2},{3,19},{19,3},{4,20},{20... | collective-permute-start | bytes 393224 | tf_op jit(solution)/shard_map/ppermute | solution.py:264
  36.5 11.1 %copy-start = (bf16[2048,256]{1,0:T(8,128)(2,1)S(1)}, bf16[2048,256]{1,0:T(8,128)(2,1)}, u32[]{:S(2)}) copy-start(bf16[2048,256]{1,0:T(8,128)(2,1)} %own_ref.1) | copy-start | bytes 3145732
  43.7 11.6 %all-to-all-start.1 = ((bf16[8,136,128]{2,1,0:T(8,128)(2,1)}), bf16[8,136,128]{2,1,0:T(8,128)(2,1)S(1)}, u32[]{:S(2)}, u32[]{:S(2)}) async-start(bf16[8,136,128]{2,1,0:T(8,128)(2,1)} %attend.1), calls=%async_computation.1 | async-start | bytes 557056 | tf_op jit(solution)/shard_map/all_to_all | solution.py:254
  47.7 26.1 %collective-permute-start.2 = (bf16[2048,256]{1,0:T(8,128)(2,1)S(1)}, bf16[2048,256]{1,0:T(8,128)(2,1)S(1)}, u32[]{:S(2)}, u32[]{:S(2)}) collective-permute-start(bf16[2048,256]{1,0:T(8,128)(2,1)S(1)} %copy-done), channel_id=1, source_target_pairs={{0,16},{16,0},{1,17},{17,1},{2,18},{18,2},{3,19},{19,3},{4,20},{20... | collective-permute-start | bytes 3145736 | tf_op jit(solution)/shard_map/ppermute | solution.py:265
